TPU v7x, 1024 devices: a whole 8x8x8 slice. The times are simulated.
1024 devices in a mesh: ctx: 64 (over y, z), head: 16 (over x, core).
Axes of the slice: x: 8, y: 8, z: 8, core: 2. Of those that a mesh axis runs over, the one named last changes fastest.
Arguments:
- queries: bfloat16 [32768, 4096], P('ctx', 'head'), may hold values from -6 to 6
- keys: bfloat16 [32768, 4096], P('ctx', 'head'), may hold values from -6 to 6
- values: bfloat16 [32768, 4096], P('ctx', 'head'), may hold values from -6 to 6
- out_grad: bfloat16 [32768, 4096], P('ctx', 'head'), may hold values from -6 to 6
- gain: float32 [4096], P('head'), may hold values from 0.5 to 1.5
- doc_lengths: int32 [64], replicated, may hold values from 1 to 8192, 32768 in all
Outputs:
- normed: bfloat16 [32768, 4096], P('ctx', 'head')
- query_grad: bfloat16 [32768, 4096], P('ctx', 'head')
- key_grad: bfloat16 [32768, 4096], P('ctx', 'head')
- value_grad: bfloat16 [32768, 4096], P('ctx', 'head')
Inputs may be any that keep to these rules, and one draw needn't show every extreme that they name: `doc_lengths`: 64 document lengths in order; the first document starts at token 0 and the lengths sum to 32768.
All inputs are finite; a program needn't handle non-finite values.
Results may differ from a plain program's by a relative error of at most 0.0053.
Values sent between devices are 32-bit elements; how exact they have to be, the bound alone decides.
No kernel may reach another device: no remote copies, remote signals or barrier semaphores. Data moves between devices by JAX's collectives and lax.ppermute only.
A program may use at most 32 MiB of HBM per device.

v0:
```python
import jax
import jax.numpy as jnp
from jax import lax
from jax.sharding import PartitionSpec as P

DH = 128
BLK = 256
FEAT = 4096


HIGHEST = lax.Precision.HIGHEST
EPSILON = 1e-06


def carried_in(part, axis, combine, identity, reverse):
    count = lax.axis_size(axis)
    place = lax.axis_index(axis)
    ahead = count - 1 - place if reverse else place
    gathered = jax.tree.map(lambda a: lax.all_gather(a, axis), part)
    state = jax.tree.map(lambda a, e: jnp.zeros_like(a) + jnp.asarray(e, a.dtype), part, identity)

    def one(lap, state):
        source = count - 1 - lap if reverse else lap
        return combine(
            state, jax.tree.map(lambda a: lax.dynamic_index_in_dim(a, source, 0, False), gathered)
        )

    return lax.fori_loop(0, ahead, one, state)


def doc_number(starts, positions):
    hits = (starts[None, :] <= positions[:, None]).astype(jnp.int32)
    return jnp.sum(hits, axis=1) - 1


def joined(earlier, later):
    return (jnp.maximum(earlier[0], later[0]), later[1] + (1.0 - later[0]) * earlier[1])


def carried(summaries, keeps, start_value, reverse):
    count = summaries.shape[0]
    visits = range(count - 1, -1, -1) if reverse else range(count)
    current = start_value
    entering = [None] * count
    for position in visits:
        entering[position] = current
        current = keeps[position] * current + summaries[position]
    return (jnp.stack(entering), current)


def masked_scores(left, right, allowed):
    scores = jnp.einsum("bthd,bshd->bhts", left, right, preferred_element_type=jnp.float32)
    return jnp.where(allowed, scores, 0.0).astype(jnp.bfloat16)


def ctx_prefix(element, identity, reverse):
    if reverse:
        return carried_in(element, "ctx", joined, identity, True)
    return carried_in(element, "ctx", joined, identity, False)


def body(queries, keys, values, out_grad, gain, doc_lengths):
    tok_count, local_width = queries.shape
    head_count = local_width // DH
    block_count = tok_count // BLK
    block_shape = (block_count, BLK, head_count, DH)
    ctx_start = lax.axis_index("ctx") * tok_count
    starts = jnp.cumsum(doc_lengths) - doc_lengths
    positions = ctx_start + jnp.arange(tok_count, dtype=jnp.int32)
    doc_tok = doc_number(starts, positions).reshape(block_count, BLK)
    edges = ctx_start + BLK * jnp.arange(block_count + 1, dtype=jnp.int32)
    doc_before = doc_number(starts, edges - 1)
    doc_at = doc_number(starts, edges)
    apply_fwd = (doc_tok == doc_before[:-1, None]).astype(jnp.float32)[:, :, None, None]
    gather_fwd = (doc_tok == doc_before[1:, None]).astype(jnp.bfloat16)[:, :, None, None]
    keep_fwd = (doc_before[1:] == doc_before[:-1]).astype(jnp.float32)
    apply_bwd = (doc_tok == doc_at[1:, None]).astype(jnp.float32)[:, :, None, None]
    gather_bwd = (doc_tok == doc_at[:-1, None]).astype(jnp.bfloat16)[:, :, None, None]
    keep_bwd = (doc_at[:-1] == doc_at[1:]).astype(jnp.float32)
    flag_fwd = (doc_before[-1] != doc_before[0]).astype(jnp.float32)
    flag_bwd = (doc_at[0] != doc_at[-1]).astype(jnp.float32)
    causal = jnp.arange(BLK)[:, None] >= jnp.arange(BLK)[None, :]
    allowed = (causal[None] & (doc_tok[:, :, None] == doc_tok[:, None, :]))[:, None]
    query_blocks = queries.reshape(block_shape)
    key_blocks = keys.reshape(block_shape)
    value_blocks = values.reshape(block_shape)
    zero_state = jnp.zeros((head_count, DH, DH), jnp.float32)
    identity = (jnp.zeros((), jnp.float32), zero_state)
    fwd_parts = jnp.einsum(
        "bshi,bshj->bhij", key_blocks * gather_fwd, value_blocks, preferred_element_type=jnp.float32
    )
    fwd_summary = carried(fwd_parts, keep_fwd, zero_state, False)[1]
    probs = masked_scores(query_blocks, key_blocks, allowed)
    flag_in, state_in = ctx_prefix((flag_fwd, fwd_summary), identity, False)
    entering = carried(fwd_parts, keep_fwd, state_in, False)[0]
    within = jnp.einsum("bhts,bshd->bthd", probs, value_blocks, preferred_element_type=jnp.float32)
    across = (
        jnp.einsum("bthi,bhij->bthj", query_blocks.astype(jnp.float32), entering, precision=HIGHEST)
        * apply_fwd
    )
    attended = (within + across).reshape(tok_count, local_width)
    scaled_grad = out_grad.astype(jnp.float32) * gain
    square_sum, inner_sum = lax.psum(
        (jnp.sum(attended * attended, axis=1), jnp.sum(scaled_grad * attended, axis=1)), "head"
    )
    radius = jnp.sqrt(square_sum / FEAT + EPSILON)
    normed = (attended / radius[:, None] * gain).astype(jnp.bfloat16)
    out_delta = (
        scaled_grad / radius[:, None] - attended * (inner_sum / (FEAT * radius**3))[:, None]
    ).astype(jnp.bfloat16)
    delta_blocks = out_delta.reshape(block_shape)
    bwd_parts = jnp.einsum(
        "bthi,bthj->bhij",
        query_blocks * gather_bwd,
        delta_blocks,
        preferred_element_type=jnp.float32,
    )
    bwd_summary = carried(bwd_parts, keep_bwd, zero_state, True)[1]
    dprobs = masked_scores(delta_blocks, value_blocks, allowed)
    flag_after, grad_after = ctx_prefix((flag_bwd, bwd_summary), identity, True)
    leaving = carried(bwd_parts, keep_bwd, grad_after, True)[0]
    query_grad = jnp.einsum(
        "bhts,bshd->bthd", dprobs, key_blocks, preferred_element_type=jnp.float32
    )
    query_grad = (
        query_grad
        + jnp.einsum(
            "bthj,bhij->bthi", delta_blocks.astype(jnp.float32), entering, precision=HIGHEST
        )
        * apply_fwd
    )
    key_grad = jnp.einsum(
        "bhts,bthd->bshd", dprobs, query_blocks, preferred_element_type=jnp.float32
    )
    key_grad = (
        key_grad
        + jnp.einsum(
            "bshj,bhij->bshi", value_blocks.astype(jnp.float32), leaving, precision=HIGHEST
        )
        * apply_bwd
    )
    value_grad = jnp.einsum(
        "bhts,bthd->bshd", probs, delta_blocks, preferred_element_type=jnp.float32
    )
    value_grad = (
        value_grad
        + jnp.einsum("bshi,bhij->bshj", key_blocks.astype(jnp.float32), leaving, precision=HIGHEST)
        * apply_bwd
    )
    return (
        normed,
        query_grad.reshape(tok_count, local_width).astype(jnp.bfloat16),
        key_grad.reshape(tok_count, local_width).astype(jnp.bfloat16),
        value_grad.reshape(tok_count, local_width).astype(jnp.bfloat16),
    )


def solution(mesh):
    return jax.shard_map(
        body,
        mesh=mesh,
        in_specs=(
            P("ctx", "head"),
            P("ctx", "head"),
            P("ctx", "head"),
            P("ctx", "head"),
            P("head"),
            P(),
        ),
        out_specs=(P("ctx", "head"), P("ctx", "head"), P("ctx", "head"), P("ctx", "head")),
        check_vma=False,
    )
```

profile of v0, /device:TPU:1, one launch (start us, length us, event | category | flops | bytes accessed | tf_op | source)
XLA Modules:
  0.0 593.7 jit_solution(13336386875966249183)
XLA Ops:
  10.0 1.0 reshape.196
  11.1 1.0 reshape.195
  13.2 1.3 slice_add_fusion.1
  14.6 1.0 reshape.194
  15.7 1.3 dynamic-slice
  19.7 130.9 %all-reduce.2 = (f32[64]{0:T(128)S(1)}, f32[64]{0:T(128)S(1)}) all-reduce(f32[64]{0:T(128)S(1)} %fusion.32, f32[64]{0:T(128)S(1)} %fusion.33), channel_id=1, replica_groups=mesh['ctx'=64,'head'=16] {'ctx'}, use_global_device_ids=true, to_apply=%add | all-reduce | flops 128 | bytes 1024
  153.1 51.5 %all-reduce.3 = (f32[512]{0:T(512)S(1)}, f32[512]{0:T(512)S(1)}) all-reduce(f32[512]{0:T(512)S(1)} %bitcast.118, f32[512]{0:T(512)S(1)} %fusion.15), channel_id=1, replica_groups=mesh['ctx'=64,'head'=16] {'head'}, use_global_device_ids=true, to_apply=%region_6.7 | all-reduce | flops 1024 | bytes 8192 | tf_op jit(solution)/shard_map/psum | solution.py:103
  206.0 1.3 slice_add_fusion
  210.0 233.7 %all-gather.5.cloned.1.call-done = f32[64,2,128,128]{3,2,1,0:T(8,128)} async-done(((f32[1,2,128,128]{3,2,1,0:T(8,128)}), f32[64,2,128,128]{3,2,1,0:T(8,128)}) %all-gather.5.cloned.1.call-update) | async-done | bytes 8388624 | tf_op jit(solution)/shard_map/all_gather | solution.py:19
  443.7 139.7 %while.27 = (s32[]{:T(128)}, f32[2,128,128]{2,1,0:T(8,128)S(1)}, s32[]{:T(128)}, f32[64,2,128,128]{3,2,1,0:T(8,128)}, f32[64]{0:T(128)S(1)}, /*index=5*/s32[]{:T(128)}, s32[]{:T(128)}, s32[]{:T(128)}, s32[]{:T(128)}, f32[1]{0:T(128)}) while((s32[]{:T(128)}, f32[2,128,128]{2,1,0:T(8,128)S(1)}, s32[]{:T(128)}, ...), condition=%wide.region_11.12_spmd, body=%wide.region_10.11_spmd.sunk | while | flops 65543 | bytes 393403 | solution.py:28
  444.9 1.0 bitcast_add_fusion.7
  447.2 1.0 bitcast_add_fusion.7
  449.4 1.0 bitcast_add_fusion.7
  451.6 1.0 bitcast_add_fusion.7
  453.8 1.0 bitcast_add_fusion.7
  456.0 1.0 bitcast_add_fusion.7
  458.2 1.0 bitcast_add_fusion.7
  460.5 1.0 bitcast_add_fusion.7
  462.7 1.0 bitcast_add_fusion.7
  464.9 1.0 bitcast_add_fusion.7
  467.1 1.0 bitcast_add_fusion.7
  469.3 1.0 bitcast_add_fusion.7
  471.6 1.0 bitcast_add_fusion.7
  473.8 1.0 bitcast_add_fusion.7
  476.0 1.0 bitcast_add_fusion.7
  478.2 1.0 bitcast_add_fusion.7
  480.4 1.0 bitcast_add_fusion.7
  482.6 1.0 bitcast_add_fusion.7
  484.9 1.0 bitcast_add_fusion.7
  487.1 1.0 bitcast_add_fusion.7
  489.3 1.0 bitcast_add_fusion.7
  491.5 1.0 bitcast_add_fusion.7
  493.7 1.0 bitcast_add_fusion.7
  495.9 1.0 bitcast_add_fusion.7
  498.2 1.0 bitcast_add_fusion.7
  500.4 1.0 bitcast_add_fusion.7
  502.6 1.0 bitcast_add_fusion.7
  504.8 1.0 bitcast_add_fusion.7
  507.0 1.0 bitcast_add_fusion.7
  509.2 1.0 bitcast_add_fusion.7
  511.5 1.0 bitcast_add_fusion.7
  513.7 1.0 bitcast_add_fusion.7
  520.3 1.0 bitcast_add_fusion.7
  522.5 1.0 bitcast_add_fusion.7
  542.5 1.0 bitcast_add_fusion.7
  544.7 1.0 bitcast_add_fusion.7
  562.4 1.0 bitcast_add_fusion.7
  564.7 1.0 bitcast_add_fusion.7
  (154 shorter events, 76.3 us)
Async XLA Ops:
  7.2 145.8 %copy-start.1 = (f32[256]{0:T(256)S(1)}, f32[256]{0:T(256)}, u32[]{:S(2)}) copy-start(f32[256]{0:T(256)} %param.14) | copy-start | bytes 3076
  7.2 145.8 %copy-start = (bf16[512,256]{1,0:T(8,128)(2,1)S(1)}, bf16[512,256]{1,0:T(8,128)(2,1)}, u32[]{:S(2)}) copy-start(bf16[512,256]{1,0:T(8,128)(2,1)} %param.13) | copy-start | bytes 786436
  7.2 144.3 %all-gather.3.cloned.1.call-start = ((), (), s32[]{:S(2)}) async-start(), calls=%async_computation | async-start | bytes 8519680 | tf_op jit(solution)/shard_map/all_gather | solution.py:19
  14.5 429.1 %all-gather.5.cloned.1.call-start = ((), (), s32[]{:S(2)}) async-start(), calls=%async_computation.1 | async-start | bytes 8519680 | tf_op jit(solution)/shard_map/all_gather | solution.py:19
Sparse Core Ops, SparseCore 0:
  14.6 119.7 all-gather.2
  207.5 236.1 all-gather.4
where the time goes:
time: 596 us; the launch traced here: 594 us
  waiting for transfers between devices  234 us (39%)
  blocking collectives  182 us (31%)
  other arithmetic  68.1 us (11%)
  local copies, waits for them, and re-layouts  47.2 us (8%)
  loops' own time  42.5 us (7%)
  between operations  15.6 us (3%)
    all_gather x2, waiting for transfers between devices, carried_in(): gathered = jax.tree.map(lambda a: lax.all_gather(a, axis), part)  234 us
    unnamed x1, blocking collectives  131 us
    add x63, other arithmetic, joined(): later[1] + (1.0 - later[0]) * earlier[1]  60.1 us
    psum x1, blocking collectives, body(): lax.psum((jnp.sum(attended * attended, axis=1), jnp.sum(scaled_grad * att...  51.5 us
    another operation x2, loops' own time, carried_in(): return lax.fori_loop(0, ahead, one, state)  42.5 us
    dynamic_slice x63, local copies, waits for them, and re-layouts, one(): lax.dynamic_index_in_dim(a, source, 0, False)  37.1 us
  transfers between devices with their start and end apart: 2, of which 1 were waited for; matrix products, arithmetic and copies ran while one was open for 1% of the time, Pallas kernels for 0%

commit v1 on v0

v1 whole, which is shorter than its diff:
```python
import functools

import jax
import jax.numpy as jnp
from jax import lax
from jax.experimental import pallas as pl
from jax.experimental.pallas import tpu as pltpu
from jax.sharding import PartitionSpec as P

DH = 128
BLK = 256
FEAT = 4096
EPSILON = 1e-06
TOK = 512
WIDE = 256
GROUP = 16
F32 = jnp.float32
BF16 = jnp.bfloat16


def dot(a, b, ca, cb):
    return lax.dot_general(a, b, (((ca,), (cb,)), ((), ())), preferred_element_type=F32)


def dot_state(a, s, cs):
    high = s.astype(BF16)
    low = (s - high.astype(F32)).astype(BF16)
    return dot(a, high, 1, cs) + dot(a, low, 1, cs)


def iota(shape, dim):
    return lax.broadcasted_iota(jnp.int32, shape, dim).astype(F32)


def doc_starts(lengths_ref):
    docs = lengths_ref.shape[1]
    lengths = jnp.broadcast_to(lengths_ref[...].astype(F32), (docs, docs))
    i, j = iota((docs, docs), 0), iota((docs, docs), 1)
    column = jnp.sum(jnp.where(j < i, lengths, 0.0), axis=1, keepdims=True)
    return jnp.sum(jnp.where(i == j, column, 0.0), axis=0, keepdims=True)


def start_of(starts, positions):
    return jnp.max(jnp.where(starts <= positions, starts, 0.0), axis=1, keepdims=True)


def first_token():
    return (lax.axis_index("ctx") * TOK).astype(F32)


def span(b):
    return slice(b * BLK, (b + 1) * BLK)


def head(h):
    return slice(h * DH, (h + 1) * DH)


def summary_kernel(lengths_ref, k_ref, v_ref, start_ref, part_ref, out_ref):
    starts = doc_starts(lengths_ref)
    rows = TOK + 8
    positions = first_token() + iota((rows, starts.shape[1]), 0)
    start_ref[...] = jnp.broadcast_to(start_of(starts, positions), (rows, DH))
    at = first_token() + iota((TOK, DH), 0)
    open_end = (at >= start_ref[TOK - 1 : TOK, :]).astype(F32)
    open_mid = (at[:BLK] >= start_ref[BLK - 1 : BLK, :]).astype(F32)
    for h in range(2):
        k = k_ref[:, head(h)].astype(F32)
        v = v_ref[:, head(h)]
        total = dot((k * open_end).astype(BF16), v, 0, 0)
        out_ref[h * 8 : (h + 1) * 8] = total.reshape(8, 16, DH)
        part_ref[head(h), :] = dot((k[:BLK] * open_mid).astype(BF16), v[:BLK], 0, 0)


def keeps(lengths_ref, reverse):
    starts = doc_starts(lengths_ref)
    group = lax.axis_index("ctx") // GROUP * GROUP
    left = (iota((GROUP, starts.shape[1]), 0) + group.astype(F32)) * TOK
    if reverse:
        return (start_of(starts, left + TOK) <= left[:, :1]).astype(F32)
    return (start_of(starts, left + (TOK - 1)) < left[:, :1]).astype(F32)


def total_kernel(reverse, lengths_ref, x_ref, out_ref):
    keep = keeps(lengths_ref, reverse)
    now = jnp.zeros(out_ref.shape, F32)
    for i in reversed(range(GROUP)) if reverse else range(GROUP):
        now = x_ref[i] + keep[i : i + 1, :] * now
    out_ref[...] = now


def prefix_kernel(reverse, lengths_ref, x_ref, before_ref, out_ref):
    keep = keeps(lengths_ref, reverse)
    now = before_ref[...]
    for i in reversed(range(GROUP)) if reverse else range(GROUP):
        out_ref[i] = now
        now = x_ref[i] + keep[i : i + 1, :] * now


def allowed(start_ref, b):
    start = start_ref[span(b), :] - (first_token() + b * BLK)
    start = jnp.concatenate([start, start], axis=1)
    t, s = iota((BLK, BLK), 0), iota((BLK, BLK), 1)
    return (s <= t) & (s >= start)


def within_kernel(start_ref, q_ref, k_ref, v_ref, probs_ref, within_ref):
    for b in range(2):
        mask = allowed(start_ref, b)
        for h in range(2):
            where = (span(b), head(h))
            scores = dot(q_ref[where], k_ref[where], 1, 1)
            probs = jnp.where(mask, scores, 0.0).astype(BF16)
            probs_ref[2 * b + h] = probs
            within_ref[where] = dot(probs, v_ref[where], 1, 0)


def entering(start_ref, state_ref, part_ref, b, h):
    state = state_ref[head(h), :]
    if b == 0:
        return state
    keep = (start_ref[BLK - 1 : BLK, :] < first_token()).astype(F32)
    return keep * state + part_ref[head(h), :]


def applies_fwd(start_ref, b):
    return (start_ref[span(b), :] < first_token() + b * BLK).astype(F32)


def attend_kernel(
    start_ref, q_ref, og_ref, gain_ref, within_ref, state_ref, part_ref, att_ref, sums_ref
):
    rows = []
    for b in range(2):
        apply = applies_fwd(start_ref, b)
        square, inner = 0.0, 0.0
        for h in range(2):
            where = (span(b), head(h))
            state = entering(start_ref, state_ref, part_ref, b, h)
            att = within_ref[where] + dot_state(q_ref[where], state, 0) * apply
            att_ref[where] = att
            scaled = og_ref[where].astype(F32) * gain_ref[:, head(h)]
            square = square + att * att
            inner = inner + scaled * att
        rows.append((square, inner))
    lines = []
    for which in range(2):
        for b in range(2):
            for c in range(2):
                piece = rows[b][which][c * DH : (c + 1) * DH]
                lines.append(jnp.sum(piece.T, axis=0, keepdims=True))
    sums = jnp.concatenate(lines, axis=0)
    for i in range(16):
        sums_ref[i] = sums


def tall(row):
    return jnp.concatenate(
        [jnp.broadcast_to(row[c : c + 1, :], (DH, DH)).T for c in range(4)], axis=0
    )


def delta_kernel(
    start_ref,
    q_ref,
    og_ref,
    gain_ref,
    att_ref,
    sums_ref,
    delta_ref,
    inverse_ref,
    part_ref,
    out_ref,
):
    sums = jnp.sum(sums_ref[...], axis=0)
    radius = jnp.sqrt(sums[:4] / FEAT + EPSILON)
    inverse = tall(1.0 / radius)
    factor = tall(sums[4:] / (FEAT * radius * radius * radius))
    inverse_ref[...] = inverse
    base = first_token()
    open_start = (start_ref[:TOK, :] <= base).astype(F32)
    open_mid = (start_ref[span(1), :] <= base + BLK).astype(F32)
    for h in range(2):
        scaled = og_ref[:, head(h)].astype(F32) * gain_ref[:, head(h)]
        delta = (scaled * inverse - att_ref[:, head(h)] * factor).astype(BF16)
        delta_ref[:, head(h)] = delta
        q = q_ref[:, head(h)].astype(F32)
        total = dot((q * open_start).astype(BF16), delta, 0, 0)
        out_ref[h * 8 : (h + 1) * 8] = total.reshape(8, 16, DH)
        part_ref[head(h), :] = dot((q[BLK:] * open_mid).astype(BF16), delta[BLK:], 0, 0)


def local_grads_kernel(
    start_ref,
    q_ref,
    k_ref,
    v_ref,
    gain_ref,
    att_ref,
    delta_ref,
    inverse_ref,
    probs_ref,
    state_ref,
    part_ref,
    normed_ref,
    qg_ref,
    kg_ref,
    vg_ref,
):
    for b in range(2):
        mask = allowed(start_ref, b)
        apply = applies_fwd(start_ref, b)
        for h in range(2):
            where = (span(b), head(h))
            normed_ref[where] = (
                att_ref[where] * inverse_ref[span(b), :] * gain_ref[:, head(h)]
            ).astype(BF16)
            delta = delta_ref[where]
            dprobs = jnp.where(mask, dot(delta, v_ref[where], 1, 1), 0.0).astype(BF16)
            state = entering(start_ref, state_ref, part_ref, b, h)
            qg_ref[where] = (
                dot(dprobs, k_ref[where], 1, 0) + dot_state(delta, state, 1) * apply
            ).astype(BF16)
            kg_ref[where] = dot(dprobs, q_ref[where], 0, 0)
            vg_ref[where] = dot(probs_ref[2 * b + h], delta, 0, 0)


def last_grads_kernel(
    start_ref, k_ref, v_ref, kg_in_ref, vg_in_ref, state_ref, part_ref, kg_ref, vg_ref
):
    base = first_token()
    keep = (start_ref[TOK : TOK + 1, :] <= base + BLK).astype(F32)
    for b in range(2):
        edge = (b + 1) * BLK
        at = base + b * BLK + iota((BLK, DH), 0)
        apply = (at >= start_ref[edge : edge + 1, :]).astype(F32)
        for h in range(2):
            where = (span(b), head(h))
            state = state_ref[head(h), :]
            if b == 0:
                state = keep * state + part_ref[head(h), :]
            kg = kg_in_ref[where] + dot_state(v_ref[where], state, 1) * apply
            vg = vg_in_ref[where] + dot_state(k_ref[where], state, 0) * apply
            kg_ref[where] = kg.astype(BF16)
            vg_ref[where] = vg.astype(BF16)


def call(kernel, outs, *args, flops=0, name=None):
    shapes = [jax.ShapeDtypeStruct(s, d) for s, d in outs]
    moved = sum(a.size * a.dtype.itemsize for a in args)
    moved += sum(s.size * s.dtype.itemsize for s in shapes)
    return pl.pallas_call(
        kernel,
        out_shape=shapes,
        compiler_params=pltpu.CompilerParams(vmem_limit_bytes=40 << 20),
        cost_estimate=pl.CostEstimate(flops=flops, bytes_accessed=moved, transcendentals=0),
        name=name,
    )(*args)


def carried(lengths, summary, reverse):
    step = -GROUP if reverse else GROUP
    count = lax.axis_size("ctx")
    groups = [list(range(g, g + GROUP)) for g in range(0, count, GROUP)]
    pairs = [(i, i + step) for i in range(count) if 0 <= i + step < count]
    piece = (GROUP, DH)
    whole = (GROUP, GROUP, DH)
    x = lax.all_to_all(summary, "ctx", 0, 0, axis_index_groups=groups)
    (total,) = call(functools.partial(total_kernel, reverse), [(piece, F32)], lengths, x)
    before = lax.ppermute(total, "ctx", pairs)
    (y,) = call(functools.partial(prefix_kernel, reverse), [(whole, F32)], lengths, x, before)
    y = lax.all_to_all(y, "ctx", 0, 0, axis_index_groups=groups)
    return y.reshape(2 * DH, DH)


def body(q, k, v, og, gain, lengths):
    lengths = lengths.reshape(1, -1)
    gain = gain.reshape(1, -1)
    tokens = (TOK, WIDE)
    states = (2 * DH, DH)
    pieces = (GROUP, GROUP, DH)
    start, part, summary = call(
        summary_kernel,
        [((TOK + 8, DH), F32), (states, F32), (pieces, F32)],
        lengths,
        k,
        v,
        flops=1 << 26,
        name="summary",
    )
    state = carried(lengths, summary, False)
    probs, within = call(
        within_kernel,
        [((4, BLK, BLK), BF16), (tokens, F32)],
        start,
        q,
        k,
        v,
        flops=1 << 28,
        name="within",
    )
    att, sums = call(
        attend_kernel,
        [(tokens, F32), ((16, 8, DH), F32)],
        start,
        q,
        og,
        gain,
        within,
        state,
        part,
        flops=1 << 27,
        name="attend",
    )
    sums = lax.all_to_all(sums, "head", 0, 0)
    delta, inverse, part_back, summary = call(
        delta_kernel,
        [(tokens, BF16), ((TOK, DH), F32), (states, F32), (pieces, F32)],
        start,
        q,
        og,
        gain,
        att,
        sums,
        flops=1 << 26,
        name="delta",
    )
    state_back = carried(lengths, summary, True)
    normed, qg, kg, vg = call(
        local_grads_kernel,
        [(tokens, BF16), (tokens, BF16), (tokens, F32), (tokens, F32)],
        start,
        q,
        k,
        v,
        gain,
        att,
        delta,
        inverse,
        probs,
        state,
        part,
        flops=1 << 29,
        name="local_grads",
    )
    kg, vg = call(
        last_grads_kernel,
        [(tokens, BF16), (tokens, BF16)],
        start,
        k,
        v,
        kg,
        vg,
        state_back,
        part_back,
        flops=1 << 28,
        name="last_grads",
    )
    return normed, qg, kg, vg


def solution(mesh):
    both = P("ctx", "head")
    return jax.shard_map(
        body,
        mesh=mesh,
        in_specs=(both, both, both, both, P("head"), P()),
        out_specs=(both, both, both, both),
        check_vma=False,
    )
```

time: 596 us -> 103 us (0.17)
  the two profiles are of different devices: /device:TPU:1 before, /device:TPU:32 now
where the time goes in v1:
time: 103 us
  blocking collectives  52.6 us (51%)
  waiting for transfers between devices  19.7 us (19%)
  starting transfers between devices  14.4 us (14%)
  Pallas kernels  7.57 us (7%)
  local copies, waits for them, and re-layouts  7.4 us (7%)
    all_to_all x2, blocking collectives, carried(): x = lax.all_to_all(summary, 'ctx', 0, 0, axis_index_groups=groups)  38.1 us
    all_to_all x1, blocking collectives, body(): sums = lax.all_to_all(sums, 'head', 0, 0)  14.5 us
    all_to_all x2, waiting for transfers between devices, carried(): y = lax.all_to_all(y, 'ctx', 0, 0, axis_index_groups=groups)  12.4 us
    pallas_call x10, Pallas kernels, call(): pl.pallas_call(kernel, out_shape=shapes, compiler_params=pltpu.CompilerPa...  7.57 us
    unnamed x32, local copies, waits for them, and re-layouts  7.4 us
    all_to_all x2, starting transfers between devices, carried(): y = lax.all_to_all(y, 'ctx', 0, 0, axis_index_groups=groups)  7.35 us
    ppermute x2, waiting for transfers between devices, carried(): before = lax.ppermute(total, 'ctx', pairs)  7.33 us
    ppermute x2, starting transfers between devices, carried(): before = lax.ppermute(total, 'ctx', pairs)  7.09 us
  transfers between devices with their start and end apart: 4, of which 4 were waited for; matrix products, arithmetic and copies ran while one was open for 0% of the time, Pallas kernels for 3%

profile of v1, /device:TPU:32, one launch (start us, length us, event | category | flops | bytes accessed | tf_op | source)
XLA Modules:
  0.0 102.5 jit_solution(7973623278539895475)
XLA Ops:
  0.6 0.0 copy-start.14
  0.6 0.6 copy-done.14
  1.3 0.0 copy-start.1
  1.3 0.9 copy-done.1
  2.2 0.0 copy-start.3
  2.2 0.9 copy-done.3
  3.2 0.5 summary.1
  3.7 0.0 copy-start.6
  3.7 0.0 copy-start.4
  3.7 26.5 %all_to_all.25.x_ref = f32[16,16,128]{2,1,0:T(8,128)S(1)} all-to-all(f32[16,16,128]{2,1,0:T(8,128)S(1)} %get-tuple-element.23), channel_id=1, replica_groups={{0,16,32,48,64,80,96,112,128,144,160,176,192,208,224,240},{256,272,288,..., dimensions={0} | all-to-all | bytes 262144 | tf_op jit(solution)/shard_map/all_to_all | solution.py:268
  30.2 0.2 shard_map.93
  30.4 0.0 copy-start
  30.4 0.0 copy-start.2
  30.4 5.2 %collective-permute-start = (f32[16,128]{1,0:T(8,128)S(1)}, f32[16,128]{1,0:T(8,128)S(1)}, u32[]{:S(2)}, u32[]{:S(2)}) collective-permute-start(f32[16,128]{1,0:T(8,128)S(1)} %shard_map.93), channel_id=1, source_target_pairs={{0,256},{16,272},{32,288},{48,304},{64,320},{80,336},{96,352},{112... | collective-permute-start | bytes 24584 | tf_op jit(solution)/shard_map/ppermute | solution.py:270
  35.6 1.4 %collective-permute-done.before_ref = f32[16,128]{1,0:T(8,128)S(1)} collective-permute-done((f32[16,128]{1,0:T(8,128)S(1)}, f32[16,128]{1,0:T(8,128)S(1)}, u32[]{:S(2)}, u32[]{:S(2)}) %collective-permute-start) | collective-permute-done | bytes 8224 | tf_op jit(solution)/shard_map/ppermute | solution.py:270
  37.0 0.9 shard_map.94
  37.9 3.5 %all-to-all-start.1 = ((f32[16,16,128]{2,1,0:T(8,128)}), f32[16,16,128]{2,1,0:T(8,128)S(1)}, u32[]{:S(2)}, u32[]{:S(2)}) async-start(f32[16,16,128]{2,1,0:T(8,128)} %shard_map.94), calls=%async_computation.1 | async-start | bytes 262144 | tf_op jit(solution)/shard_map/all_to_all | solution.py:272
  41.4 0.0 copy-done.4
  41.4 0.0 copy-done
  41.4 0.0 copy-done.2
  41.4 0.0 copy-start.5
  41.4 0.7 within.1
  42.1 7.8 %all-to-all-done.1 = f32[16,16,128]{2,1,0:T(8,128)S(1)} async-done(((f32[16,16,128]{2,1,0:T(8,128)}), f32[16,16,128]{2,1,0:T(8,128)S(1)}, u32[]{:S(2)}, u32[]{:S(2)}) %all-to-all-start.1) | async-done | bytes 131104 | tf_op jit(solution)/shard_map/all_to_all | solution.py:272
  49.9 0.0 copy-start.15
  49.9 0.0 copy-done.6
  49.9 0.0 copy-done.5
  49.9 0.7 copy-done.15
  50.6 0.4 attend.1
  51.0 14.5 %all_to_all.26.sums_ref = f32[16,8,128]{2,1,0:T(8,128)S(1)} all-to-all(f32[16,8,128]{2,1,0:T(8,128)S(1)} %get-tuple-element.26), channel_id=1, replica_groups=mesh['ctx'=64,'head'=16] {'head'}, dimensions={0} | all-to-all | bytes 131072 | tf_op jit(solution)/shard_map/all_to_all | solution.py:315
  65.6 0.5 delta.1
  66.1 0.0 copy-start.10
  66.1 0.7 copy-done.10
  66.8 0.6 copy-done.12
  67.4 11.6 %all_to_all.27.x_ref = f32[16,16,128]{2,1,0:T(8,128)S(1)} all-to-all(f32[16,16,128]{2,1,0:T(8,128)S(1)} %get-tuple-element.34), channel_id=1, replica_groups={{0,16,32,48,64,80,96,112,128,144,160,176,192,208,224,240},{256,272,288,..., dimensions={0} | all-to-all | bytes 262144 | tf_op jit(solution)/shard_map/all_to_all | solution.py:268
  79.1 0.2 shard_map.95
  79.3 1.9 %collective-permute-start.1 = (f32[16,128]{1,0:T(8,128)S(1)}, f32[16,128]{1,0:T(8,128)S(1)}, u32[]{:S(2)}, u32[]{:S(2)}) collective-permute-start(f32[16,128]{1,0:T(8,128)S(1)} %shard_map.95), channel_id=1, source_target_pairs={{256,0},{272,16},{288,32},{304,48},{320,64},{336,80},{352,96},{368... | collective-permute-start | bytes 24584 | tf_op jit(solution)/shard_map/ppermute | solution.py:270
  81.2 5.9 %collective-permute-done.1.before_ref = f32[16,128]{1,0:T(8,128)S(1)} collective-permute-done((f32[16,128]{1,0:T(8,128)S(1)}, f32[16,128]{1,0:T(8,128)S(1)}, u32[]{:S(2)}, u32[]{:S(2)}) %collective-permute-start.1) | collective-permute-done | bytes 8224 | tf_op jit(solution)/shard_map/ppermute | solution.py:270
  87.1 0.0 copy-done.8
  87.1 0.8 shard_map.96
  88.0 3.8 %all-to-all-start.4 = ((f32[16,16,128]{2,1,0:T(8,128)}), f32[16,16,128]{2,1,0:T(8,128)S(1)}, u32[]{:S(2)}, u32[]{:S(2)}) async-start(f32[16,16,128]{2,1,0:T(8,128)} %shard_map.96), calls=%async_computation.4 | async-start | bytes 262144 | tf_op jit(solution)/shard_map/all_to_all | solution.py:272
  91.8 0.0 copy-done.7
  91.8 0.0 copy-start.9
  91.9 0.9 copy-done.9
  92.8 0.9 copy-done.11
  93.7 2.1 %local_grads.1 = (bf16[512,256]{1,0:T(8,128)(2,1)}, bf16[512,256]{1,0:T(8,128)(2,1)}, f32[512,256]{1,0:T(8,128)S(1)}, f32[512,256]{1,0:T(8,128)S(1)}) custom-call(f32[520,128]{1,0:T(8,128)S(1)} %get-tuple-element.21.start_ref, bf16[512,256]{1,0:T(8,128)(2,1)S(1)} %copy-done, bf16[512,256]{1,0:T(8,128)(2,1)S(1)} %copy-done.2, bf16[512,256]{1,0:T(8,128)(2,1)S(1)} %copy-done.4, ...), custom_call_target="tpu_custom_call" | custom-call | flops 536870912 | bytes 4461568 | tf_op jit(solution)/shard_map/local_grads/pallas_call | solution.py:252
  95.9 4.5 %all-to-all-done.4 = f32[16,16,128]{2,1,0:T(8,128)S(1)} async-done(((f32[16,16,128]{2,1,0:T(8,128)}), f32[16,16,128]{2,1,0:T(8,128)S(1)}, u32[]{:S(2)}, u32[]{:S(2)}) %all-to-all-start.4) | async-done | bytes 131104 | tf_op jit(solution)/shard_map/all_to_all | solution.py:272
  100.4 0.9 copy-done.13
  101.3 1.2 %last_grads.1 = (bf16[512,256]{1,0:T(8,128)(2,1)}, bf16[512,256]{1,0:T(8,128)(2,1)}) custom-call(f32[520,128]{1,0:T(8,128)S(1)} %get-tuple-element.21.start_ref, bf16[512,256]{1,0:T(8,128)(2,1)S(1)} %copy-done.2, bf16[512,256]{1,0:T(8,128)(2,1)S(1)} %copy-done.4, f32[512,256]{1,0:T(8,128)S(1)} %get-tuple-element.32.kg_in_ref, ...), custom_call_target="tpu_custom_call" | custom-call | flops 268435456 | bytes 2625536 | tf_op jit(solution)/shard_map/last_grads/pallas_call | solution.py:252
  (5 shorter events, 0.0 us)
Async XLA Ops:
  0.6 0.7 copy-start.14
  1.3 0.9 copy-start.1
  2.2 0.9 copy-start.3
  3.7 46.2 %copy-start.6 = (f32[256,128]{1,0:T(8,128)}, f32[256,128]{1,0:T(8,128)S(1)}, u32[]{:S(2)}) copy-start(f32[256,128]{1,0:T(8,128)S(1)} %get-tuple-element.24.part_ref) | copy-start | bytes 393220
  3.7 37.7 %copy-start.4 = (bf16[512,256]{1,0:T(8,128)(2,1)S(1)}, bf16[512,256]{1,0:T(8,128)(2,1)}, u32[]{:S(2)}) copy-start(bf16[512,256]{1,0:T(8,128)(2,1)} %v_ref.7) | copy-start | bytes 786436
  30.4 11.0 %copy-start = (bf16[512,256]{1,0:T(8,128)(2,1)S(1)}, bf16[512,256]{1,0:T(8,128)(2,1)}, u32[]{:S(2)}) copy-start(bf16[512,256]{1,0:T(8,128)(2,1)} %q_ref.7) | copy-start | bytes 786436
  30.4 11.0 %copy-start.2 = (bf16[512,256]{1,0:T(8,128)(2,1)S(1)}, bf16[512,256]{1,0:T(8,128)(2,1)}, u32[]{:S(2)}) copy-start(bf16[512,256]{1,0:T(8,128)(2,1)} %k_ref.7) | copy-start | bytes 786436
  30.4 6.6 %collective-permute-start = (f32[16,128]{1,0:T(8,128)S(1)}, f32[16,128]{1,0:T(8,128)S(1)}, u32[]{:S(2)}, u32[]{:S(2)}) collective-permute-start(f32[16,128]{1,0:T(8,128)S(1)} %shard_map.93), channel_id=1, source_target_pairs={{0,256},{16,272},{32,288},{48,304},{64,320},{80,336},{96,352},{112... | collective-permute-start | bytes 24584 | tf_op jit(solution)/shard_map/ppermute | solution.py:270
  37.9 12.0 %all-to-all-start.1 = ((f32[16,16,128]{2,1,0:T(8,128)}), f32[16,16,128]{2,1,0:T(8,128)S(1)}, u32[]{:S(2)}, u32[]{:S(2)}) async-start(f32[16,16,128]{2,1,0:T(8,128)} %shard_map.94), calls=%async_computation.1 | async-start | bytes 262144 | tf_op jit(solution)/shard_map/all_to_all | solution.py:272
  41.4 8.5 %copy-start.5 = (bf16[512,256]{1,0:T(8,128)(2,1)S(1)}, bf16[512,256]{1,0:T(8,128)(2,1)}, u32[]{:S(2)}) copy-start(bf16[512,256]{1,0:T(8,128)(2,1)} %og_ref.3) | copy-start | bytes 786436
  49.9 0.7 copy-start.15
  66.1 0.7 copy-start.10
  66.8 0.6 copy-start.12
  67.4 19.7 %copy-start.8 = (bf16[512,256]{1,0:T(8,128)(2,1)}, bf16[512,256]{1,0:T(8,128)(2,1)S(1)}, u32[]{:S(2)}) copy-start(bf16[512,256]{1,0:T(8,128)(2,1)S(1)} %get-tuple-element.27.delta_ref) | copy-start | bytes 786436
  79.3 7.9 %collective-permute-start.1 = (f32[16,128]{1,0:T(8,128)S(1)}, f32[16,128]{1,0:T(8,128)S(1)}, u32[]{:S(2)}, u32[]{:S(2)}) collective-permute-start(f32[16,128]{1,0:T(8,128)S(1)} %shard_map.95), channel_id=1, source_target_pairs={{256,0},{272,16},{288,32},{304,48},{320,64},{336,80},{352,96},{368... | collective-permute-start | bytes 24584 | tf_op jit(solution)/shard_map/ppermute | solution.py:270
  88.0 3.8 %copy-start.7 = (f32[256,128]{1,0:T(8,128)S(1)}, f32[256,128]{1,0:T(8,128)}, u32[]{:S(2)}) copy-start(f32[256,128]{1,0:T(8,128)} %copy-done.6) | copy-start | bytes 393220
  88.0 12.4 %all-to-all-start.4 = ((f32[16,16,128]{2,1,0:T(8,128)}), f32[16,16,128]{2,1,0:T(8,128)S(1)}, u32[]{:S(2)}, u32[]{:S(2)}) async-start(f32[16,16,128]{2,1,0:T(8,128)} %shard_map.96), calls=%async_computation.4 | async-start | bytes 262144 | tf_op jit(solution)/shard_map/all_to_all | solution.py:272
  91.8 1.0 copy-start.9
  92.8 0.9 copy-start.11
  100.4 0.9 copy-start.13

commit v2 on v1

v2 whole, which is shorter than its diff:
```python
import functools

import jax
import jax.numpy as jnp
from jax import lax
from jax.experimental import pallas as pl
from jax.experimental.pallas import tpu as pltpu
from jax.sharding import PartitionSpec as P

DH = 128
BLK = 256
FEAT = 4096
EPSILON = 1e-06
TOK = 512
WIDE = 256
CHUNK = 256
GROUP = 16
F32 = jnp.float32
BF16 = jnp.bfloat16


def dot(a, b, ca, cb):
    return lax.dot_general(a, b, (((ca,), (cb,)), ((), ())), preferred_element_type=F32)


def dot_state(a, s, cs):
    high = s.astype(BF16)
    low = (s - high.astype(F32)).astype(BF16)
    return dot(a, high, 1, cs) + dot(a, low, 1, cs)


def iota(shape, dim):
    return lax.broadcasted_iota(jnp.int32, shape, dim).astype(F32)


def doc_starts(lengths_ref):
    docs = lengths_ref.shape[1]
    lengths = jnp.broadcast_to(lengths_ref[...].astype(F32), (docs, docs))
    i, j = iota((docs, docs), 0), iota((docs, docs), 1)
    column = jnp.sum(jnp.where(j < i, lengths, 0.0), axis=1, keepdims=True)
    return jnp.sum(jnp.where(i == j, column, 0.0), axis=0, keepdims=True)


def start_of(starts, positions):
    return jnp.max(jnp.where(starts <= positions, starts, 0.0), axis=1, keepdims=True)


def first_token():
    return (lax.axis_index("ctx") * TOK).astype(F32)


def span(b):
    return slice(b * BLK, (b + 1) * BLK)


def head(h):
    return slice(h * DH, (h + 1) * DH)


def summary_kernel(lengths_hbm, k_hbm, v_hbm, out_ref, lengths, k_in, v_in, sems):
    parts = range(0, TOK, CHUNK)
    first = pltpu.make_async_copy(lengths_hbm, lengths, sems.at[0])
    first.start()
    copies = []
    for n, at in enumerate(parts):
        rows = slice(at, at + CHUNK)
        for m, (hbm, ref) in enumerate(((k_hbm, k_in), (v_hbm, v_in))):
            copy = pltpu.make_async_copy(hbm.at[rows], ref.at[rows], sems.at[1 + 2 * n + m])
            copy.start()
            copies.append(copy)
    first.wait()
    starts = doc_starts(lengths)
    last = jnp.broadcast_to(first_token() + (TOK - 1), (8, starts.shape[1]))
    start = start_of(starts, last)[:1] - first_token()
    totals = [0.0, 0.0]
    for n, at in enumerate(parts):
        copies[2 * n].wait()
        copies[2 * n + 1].wait()
        rows = slice(at, at + CHUNK)
        open_end = (iota((CHUNK, DH), 0) + at >= start).astype(F32)
        for h in range(2):
            k = k_in[rows, head(h)].astype(F32)
            totals[h] = totals[h] + dot((k * open_end).astype(BF16), v_in[rows, head(h)], 0, 0)
    for h in range(2):
        out_ref[h * 8 : (h + 1) * 8] = totals[h].reshape(8, 16, DH)


def keeps(starts, reverse):
    group = lax.axis_index("ctx") // GROUP * GROUP
    left = (iota((GROUP, starts.shape[1]), 0) + group.astype(F32)) * TOK
    if reverse:
        return (start_of(starts, left + TOK) <= left[:, :1]).astype(F32)
    return (start_of(starts, left + (TOK - 1)) < left[:, :1]).astype(F32)


def order(reverse):
    return reversed(range(GROUP)) if reverse else range(GROUP)


def total_kernel(reverse, lengths_ref, x_ref, out_ref):
    keep = keeps(doc_starts(lengths_ref), reverse)
    now = jnp.zeros(out_ref.shape, F32)
    for i in order(reverse):
        now = x_ref[i] + keep[i : i + 1, :] * now
    out_ref[...] = now


def group_prefix(reverse, starts, x_ref, prefix_ref, open_ref):
    keep = keeps(starts, reverse)
    now = jnp.zeros(x_ref.shape[1:], F32)
    still = jnp.ones((1, DH), F32)
    for i in order(reverse):
        prefix_ref[i] = now
        open_ref[i : i + 1, :] = still
        now = x_ref[i] + keep[i : i + 1, :] * now
        still = keep[i : i + 1, :] * still


def join_kernel(prefix_ref, open_ref, before_ref, out_ref):
    before = before_ref[...]
    for i in range(GROUP):
        out_ref[i] = prefix_ref[i] + open_ref[i : i + 1, :] * before


def allowed(start_ref, b):
    start = start_ref[span(b), :] - (first_token() + b * BLK)
    start = jnp.concatenate([start, start], axis=1)
    t, s = iota((BLK, BLK), 0), iota((BLK, BLK), 1)
    return (s <= t) & (s >= start)


def within_kernel(
    lengths_ref,
    x_ref,
    q_ref,
    k_ref,
    v_ref,
    og_ref,
    gain_ref,
    prefix_ref,
    open_ref,
    start_ref,
    probs_ref,
    within_ref,
    scaled_ref,
    part_ref,
):
    starts = doc_starts(lengths_ref)
    group_prefix(False, starts, x_ref, prefix_ref, open_ref)
    positions = first_token() + iota((TOK + 8, starts.shape[1]), 0)
    start_ref[...] = jnp.broadcast_to(start_of(starts, positions), start_ref.shape)
    at = first_token() + iota((BLK, DH), 0)
    open_mid = (at >= start_ref[BLK - 1 : BLK, :]).astype(F32)
    for h in range(2):
        k = k_ref[:BLK, head(h)].astype(F32)
        part_ref[head(h), :] = dot((k * open_mid).astype(BF16), v_ref[:BLK, head(h)], 0, 0)
    for b in range(2):
        mask = allowed(start_ref, b)
        for h in range(2):
            where = (span(b), head(h))
            scores = dot(q_ref[where], k_ref[where], 1, 1)
            probs = jnp.where(mask, scores, 0.0).astype(BF16)
            probs_ref[2 * b + h] = probs
            within_ref[where] = dot(probs, v_ref[where], 1, 0)
            scaled_ref[where] = og_ref[where].astype(F32) * gain_ref[:, head(h)]


def entering(start_ref, state_ref, part_ref, b, h):
    state = state_ref[head(h), :]
    if b == 0:
        return state
    keep = (start_ref[BLK - 1 : BLK, :] < first_token()).astype(F32)
    return keep * state + part_ref[head(h), :]


def applies_fwd(start_ref, b):
    return (start_ref[span(b), :] < first_token() + b * BLK).astype(F32)


def attend_kernel(
    start_ref, q_ref, scaled_ref, within_ref, state_ref, part_ref, att_ref, sums_ref
):
    rows = []
    for b in range(2):
        apply = applies_fwd(start_ref, b)
        square, inner = 0.0, 0.0
        for h in range(2):
            where = (span(b), head(h))
            state = entering(start_ref, state_ref, part_ref, b, h)
            att = within_ref[where] + dot_state(q_ref[where], state, 0) * apply
            att_ref[where] = att
            scaled = scaled_ref[where]
            square = square + att * att
            inner = inner + scaled * att
        rows.append((square, inner))
    lines = []
    for which in range(2):
        for b in range(2):
            for c in range(2):
                piece = rows[b][which][c * DH : (c + 1) * DH]
                lines.append(jnp.sum(piece.T, axis=0, keepdims=True))
    sums = jnp.concatenate(lines, axis=0)
    for i in range(16):
        sums_ref[i] = sums


def tall(row):
    return jnp.concatenate(
        [jnp.broadcast_to(row[c : c + 1, :], (DH, DH)).T for c in range(4)], axis=0
    )


def delta_kernel(start_ref, q_ref, scaled_ref, att_ref, sums_ref, delta_ref, out_ref):
    sums = jnp.sum(sums_ref[...], axis=0)
    radius = jnp.sqrt(sums[:4] / FEAT + EPSILON)
    inverse = tall(1.0 / radius)
    factor = tall(sums[4:] / (FEAT * radius * radius * radius))
    open_start = (start_ref[:TOK, :] <= first_token()).astype(F32)
    for h in range(2):
        delta = scaled_ref[:, head(h)] * inverse - att_ref[:, head(h)] * factor
        delta = delta.astype(BF16)
        delta_ref[:, head(h)] = delta
        q = q_ref[:, head(h)].astype(F32)
        total = dot((q * open_start).astype(BF16), delta, 0, 0)
        out_ref[h * 8 : (h + 1) * 8] = total.reshape(8, 16, DH)


def local_grads_kernel(
    lengths_ref,
    start_ref,
    x_ref,
    q_ref,
    k_ref,
    v_ref,
    gain_ref,
    att_ref,
    delta_ref,
    sums_ref,
    probs_ref,
    state_ref,
    part_ref,
    prefix_ref,
    open_ref,
    normed_ref,
    qg_ref,
    kg_ref,
    vg_ref,
    back_ref,
):
    group_prefix(True, doc_starts(lengths_ref), x_ref, prefix_ref, open_ref)
    sums = jnp.sum(sums_ref[...], axis=0)
    inverse = tall(1.0 / jnp.sqrt(sums[:4] / FEAT + EPSILON))
    open_mid = (start_ref[span(1), :] <= first_token() + BLK).astype(F32)
    for h in range(2):
        q = q_ref[BLK:, head(h)].astype(F32)
        back_ref[head(h), :] = dot((q * open_mid).astype(BF16), delta_ref[BLK:, head(h)], 0, 0)
    for b in range(2):
        mask = allowed(start_ref, b)
        apply = applies_fwd(start_ref, b)
        for h in range(2):
            where = (span(b), head(h))
            normed_ref[where] = (att_ref[where] * inverse[span(b)] * gain_ref[:, head(h)]).astype(
                BF16
            )
            delta = delta_ref[where]
            dprobs = jnp.where(mask, dot(delta, v_ref[where], 1, 1), 0.0).astype(BF16)
            state = entering(start_ref, state_ref, part_ref, b, h)
            qg_ref[where] = (
                dot(dprobs, k_ref[where], 1, 0) + dot_state(delta, state, 1) * apply
            ).astype(BF16)
            kg_ref[where] = dot(dprobs, q_ref[where], 0, 0)
            vg_ref[where] = dot(probs_ref[2 * b + h], delta, 0, 0)


def last_grads_kernel(
    start_ref,
    k_ref,
    v_ref,
    kg_in_ref,
    vg_in_ref,
    state_ref,
    part_ref,
    kg_hbm,
    vg_hbm,
    kg_ref,
    vg_ref,
    sems,
):
    base = first_token()
    keep = (start_ref[TOK : TOK + 1, :] <= base + BLK).astype(F32)
    copies = []
    for b in range(2):
        edge = (b + 1) * BLK
        at = base + b * BLK + iota((BLK, DH), 0)
        apply = (at >= start_ref[edge : edge + 1, :]).astype(F32)
        for h in range(2):
            where = (span(b), head(h))
            state = state_ref[head(h), :]
            if b == 0:
                state = keep * state + part_ref[head(h), :]
            kg = kg_in_ref[where] + dot_state(v_ref[where], state, 1) * apply
            vg = vg_in_ref[where] + dot_state(k_ref[where], state, 0) * apply
            kg_ref[where] = kg.astype(BF16)
            vg_ref[where] = vg.astype(BF16)
        for i, (ref, hbm) in enumerate(((kg_ref, kg_hbm), (vg_ref, vg_hbm))):
            copy = pltpu.make_async_copy(ref.at[span(b)], hbm.at[span(b)], sems.at[b, i])
            copy.start()
            copies.append(copy)
    for copy in copies:
        copy.wait()


def call(kernel, outs, *args, flops=0, name=None, grant=24, bound=True, **rest):
    shapes = [jax.ShapeDtypeStruct(s, d) for s, d in outs]
    moved = sum(a.size * a.dtype.itemsize for a in args)
    moved += sum(s.size * s.dtype.itemsize for s in shapes)
    moved = moved if bound else 0
    return pl.pallas_call(
        kernel,
        out_shape=shapes,
        compiler_params=pltpu.CompilerParams(vmem_limit_bytes=grant << 20),
        cost_estimate=pl.CostEstimate(flops=flops, bytes_accessed=moved, transcendentals=0),
        name=name,
        **rest,
    )(*args)


HBM = pl.BlockSpec(memory_space=pltpu.HBM)
VMEM = pl.BlockSpec(memory_space=pltpu.VMEM)
TOKENS = (TOK, WIDE)
STATES = (2 * DH, DH)
PIECE = (GROUP, DH)
PIECES = (GROUP, GROUP, DH)


def swap(x):
    count = lax.axis_size("ctx")
    groups = [list(range(g, g + GROUP)) for g in range(0, count, GROUP)]
    return lax.all_to_all(x, "ctx", 0, 0, axis_index_groups=groups)


def total_before(lengths, x, reverse):
    step = -GROUP if reverse else GROUP
    count = lax.axis_size("ctx")
    pairs = [(i, i + step) for i in range(count) if 0 <= i + step < count]
    kernel = functools.partial(total_kernel, reverse)
    (total,) = call(kernel, [(PIECE, F32)], lengths, x, name="total")
    return lax.ppermute(total, "ctx", pairs)


def joined(prefix, still, before):
    (y,) = call(join_kernel, [(PIECES, F32)], prefix, still, before, name="join")
    return swap(y).reshape(STATES)


def body(q, k, v, og, gain, lengths):
    lengths = lengths.reshape(1, -1)
    gain = gain.reshape(1, -1)
    docs = lengths.shape
    (summary,) = call(
        summary_kernel,
        [(PIECES, F32)],
        lengths,
        k,
        v,
        flops=1 << 26,
        name="summary",
        grant=60,
        in_specs=[HBM] * 3,
        scratch_shapes=[
            pltpu.VMEM(docs, jnp.int32),
            pltpu.VMEM(TOKENS, BF16),
            pltpu.VMEM(TOKENS, BF16),
            pltpu.SemaphoreType.DMA((1 + 2 * (TOK // CHUNK),)),
        ],
    )
    x = swap(summary)
    before = total_before(lengths, x, False)
    prefix, still, start, probs, within, scaled, part = call(
        within_kernel,
        [
            (PIECES, F32),
            (PIECE, F32),
            ((TOK + 8, DH), F32),
            ((4, BLK, BLK), BF16),
            (TOKENS, F32),
            (TOKENS, F32),
            (STATES, F32),
        ],
        lengths,
        x,
        q,
        k,
        v,
        og,
        gain,
        flops=1 << 28,
        name="within",
    )
    state = joined(prefix, still, before)
    att, sums = call(
        attend_kernel,
        [(TOKENS, F32), ((16, 8, DH), F32)],
        start,
        q,
        scaled,
        within,
        state,
        part,
        flops=1 << 27,
        name="attend",
    )
    sums = lax.all_to_all(sums, "head", 0, 0)
    delta, summary = call(
        delta_kernel,
        [(TOKENS, BF16), (PIECES, F32)],
        start,
        q,
        scaled,
        att,
        sums,
        flops=1 << 26,
        name="delta",
    )
    x = swap(summary)
    before = total_before(lengths, x, True)
    prefix, still, normed, qg, kg, vg, part_back = call(
        local_grads_kernel,
        [
            (PIECES, F32),
            (PIECE, F32),
            (TOKENS, BF16),
            (TOKENS, BF16),
            (TOKENS, F32),
            (TOKENS, F32),
            (STATES, F32),
        ],
        lengths,
        start,
        x,
        q,
        k,
        v,
        gain,
        att,
        delta,
        sums,
        probs,
        state,
        part,
        flops=1 << 29,
        name="local_grads",
    )
    state_back = joined(prefix, still, before)
    kg, vg = call(
        last_grads_kernel,
        [(TOKENS, BF16), (TOKENS, BF16)],
        start,
        k,
        v,
        kg,
        vg,
        state_back,
        part_back,
        flops=1 << 28,
        name="last_grads",
        in_specs=[VMEM] * 7,
        out_specs=[HBM] * 2,
        scratch_shapes=[
            pltpu.VMEM(TOKENS, BF16),
            pltpu.VMEM(TOKENS, BF16),
            pltpu.SemaphoreType.DMA((2, 2)),
        ],
    )
    return normed, qg, kg, vg


def solution(mesh):
    both = P("ctx", "head")
    return jax.shard_map(
        body,
        mesh=mesh,
        in_specs=(both, both, both, both, P("head"), P()),
        out_specs=(both, both, both, both),
        check_vma=False,
    )
```

time: 103 us -> 96.7 us (0.939)
  blocking collectives: 52.6 us -> 76.5 us
  waiting for transfers between devices: 19.7 us -> 4.22 us
  starting transfers between devices: 14.4 us -> 6.96 us
  local copies, waits for them, and re-layouts: 7.4 us -> 0.03 us
    all_to_all x2 -> x4, blocking collectives: 38.1 us -> 62 us  [swap(): return lax.all_to_all(x, 'ctx', 0, 0, axis_index_groups=groups)]
    all_to_all x2 -> x0, waiting for transfers between devices: 12.4 us -> none  [carried(): y = lax.all_to_all(y, 'ctx', 0, 0, axis_index_groups=groups)]
    unnamed x32 -> x12, local copies, waits for them, and re-layouts: 7.4 us -> 0.03 us
    all_to_all x2 -> x0, starting transfers between devices: 7.35 us -> none  [carried(): y = lax.all_to_all(y, 'ctx', 0, 0, axis_index_groups=groups)]
    ppermute x2, waiting for transfers between devices: 7.33 us -> 4.22 us  [total_before(): return lax.ppermute(total, 'ctx', pairs)]
  transfers between devices with their start and end apart: 4 -> 2, of which waited for: 4 -> 2; matrix products, arithmetic and copies ran while one was open for 0% -> 0% of each run, Pallas kernels for 3% -> 3%
where the time goes in v2:
time: 96.7 us; the launch traced here: 96.3 us
  blocking collectives  76.5 us (79%)
  Pallas kernels  7.81 us (8%)
  starting transfers between devices  6.96 us (7%)
  waiting for transfers between devices  4.22 us (4%)
    all_to_all x4, blocking collectives, swap(): return lax.all_to_all(x, 'ctx', 0, 0, axis_index_groups=groups)  62 us
    all_to_all x1, blocking collectives, body(): sums = lax.all_to_all(sums, 'head', 0, 0)  14.5 us
    pallas_call x10, Pallas kernels, call(): pl.pallas_call(kernel, out_shape=shapes, compiler_params=pltpu.CompilerPa...  7.81 us
    ppermute x2, starting transfers between devices, total_before(): return lax.ppermute(total, 'ctx', pairs)  6.96 us
    ppermute x2, waiting for transfers between devices, total_before(): return lax.ppermute(total, 'ctx', pairs)  4.22 us
  transfers between devices with their start and end apart: 2, of which 2 were waited for; matrix products, arithmetic and copies ran while one was open for 0% of the time, Pallas kernels for 3%

profile of v2, /device:TPU:32, one launch (start us, length us, event | category | flops | bytes accessed | tf_op | source)
XLA Modules:
  0.0 96.3 jit_solution(744780658267688708)
XLA Ops:
  0.6 0.0 copy-start.4
  0.6 0.0 copy-start.1
  0.7 0.0 copy-start.2
  0.7 0.0 copy-start.3
  0.7 2.2 %summary.1 = f32[16,16,128]{2,1,0:T(8,128)} custom-call(s32[1,64]{1,0:T(1,128)} %bitcast.7, bf16[512,256]{1,0:T(8,128)(2,1)} %k_ref.5, bf16[512,256]{1,0:T(8,128)(2,1)} %v_ref.5), custom_call_target="tpu_custom_call" | custom-call | flops 67108864 | bytes 655616 | tf_op jit(solution)/shard_map/summary/pallas_call | solution.py:318
  2.8 0.0 copy-start
  2.9 26.7 %all_to_all.25.x_ref = f32[16,16,128]{2,1,0:T(8,128)S(1)} all-to-all(f32[16,16,128]{2,1,0:T(8,128)} %summary.1), channel_id=1, replica_groups={{0,16,32,48,64,80,96,112,128,144,160,176,192,208,224,240},{256,272,288,..., dimensions={0} | all-to-all | bytes 262144 | tf_op jit(solution)/shard_map/all_to_all | solution.py:339
  29.5 0.0 copy-done.4
  29.6 0.2 total.2
  29.8 0.0 copy-start.5
  29.8 5.0 %collective-permute-start = (f32[16,128]{1,0:T(8,128)S(1)}, f32[16,128]{1,0:T(8,128)S(1)}, u32[]{:S(2)}, u32[]{:S(2)}) collective-permute-start(f32[16,128]{1,0:T(8,128)S(1)} %total.2), channel_id=1, source_target_pairs={{0,256},{16,272},{32,288},{48,304},{64,320},{80,336},{96,352},{112... | collective-permute-start | bytes 24584 | tf_op jit(solution)/shard_map/ppermute | solution.py:348
  34.8 0.0 copy-done.1
  34.8 0.0 copy-done.2
  34.8 0.0 copy-done.3
  34.8 0.0 copy-done
  34.9 0.0 copy-done.5
  34.9 0.8 within.1
  35.7 0.5 collective-permute-done.before_ref
  36.2 11.6 %all_to_all.26 = f32[16,16,128]{2,1,0:T(8,128)S(1)} all-to-all(f32[16,16,128]{2,1,0:T(8,128)S(1)} %join.2), channel_id=1, replica_groups={{0,16,32,48,64,80,96,112,128,144,160,176,192,208,224,240},{256,272,288,..., dimensions={0} | all-to-all | bytes 262144 | tf_op jit(solution)/shard_map/all_to_all | solution.py:339
  47.8 0.4 attend.1
  48.2 14.5 %all_to_all.27.sums_ref = f32[16,8,128]{2,1,0:T(8,128)S(1)} all-to-all(f32[16,8,128]{2,1,0:T(8,128)S(1)} %get-tuple-element.31), channel_id=1, replica_groups=mesh['ctx'=64,'head'=16] {'head'}, dimensions={0} | all-to-all | bytes 131072 | tf_op jit(solution)/shard_map/all_to_all | solution.py:413
  62.8 0.5 delta.1
  63.3 11.7 %all_to_all.28.x_ref = f32[16,16,128]{2,1,0:T(8,128)S(1)} all-to-all(f32[16,16,128]{2,1,0:T(8,128)S(1)} %get-tuple-element.32), channel_id=1, replica_groups={{0,16,32,48,64,80,96,112,128,144,160,176,192,208,224,240},{256,272,288,..., dimensions={0} | all-to-all | bytes 262144 | tf_op jit(solution)/shard_map/all_to_all | solution.py:339
  75.0 0.2 total.3
  75.2 1.9 %collective-permute-start.1 = (f32[16,128]{1,0:T(8,128)S(1)}, f32[16,128]{1,0:T(8,128)S(1)}, u32[]{:S(2)}, u32[]{:S(2)}) collective-permute-start(f32[16,128]{1,0:T(8,128)S(1)} %total.3), channel_id=1, source_target_pairs={{256,0},{272,16},{288,32},{304,48},{320,64},{336,80},{352,96},{368... | collective-permute-start | bytes 24584 | tf_op jit(solution)/shard_map/ppermute | solution.py:348
  77.1 2.3 %local_grads.1 = (f32[16,16,128]{2,1,0:T(8,128)S(1)}, f32[16,128]{1,0:T(8,128)S(1)}, bf16[512,256]{1,0:T(8,128)(2,1)}, bf16[512,256]{1,0:T(8,128)(2,1)}, f32[512...) custom-call(s32[1,64]{1,0:T(1,128)S(1)} %bitcast.11, f32[520,128]{1,0:T(8,128)S(1)} %get-tuple-element.24.start_ref, ...), custom_call_target="tpu_custom_call" | custom-call | flops 536870912 | bytes 4666624 | tf_op jit(solution)/shard_map/local_grads/pallas_call | solution.py:318
  79.4 3.7 %collective-permute-done.1.before_ref = f32[16,128]{1,0:T(8,128)S(1)} collective-permute-done((f32[16,128]{1,0:T(8,128)S(1)}, f32[16,128]{1,0:T(8,128)S(1)}, u32[]{:S(2)}, u32[]{:S(2)}) %collective-permute-start.1) | collective-permute-done | bytes 8224 | tf_op jit(solution)/shard_map/ppermute | solution.py:348
  83.1 12.1 %all_to_all.29 = f32[16,16,128]{2,1,0:T(8,128)S(1)} all-to-all(f32[16,16,128]{2,1,0:T(8,128)S(1)} %join.3), channel_id=1, replica_groups={{0,16,32,48,64,80,96,112,128,144,160,176,192,208,224,240},{256,272,288,..., dimensions={0} | all-to-all | bytes 262144 | tf_op jit(solution)/shard_map/all_to_all | solution.py:339
  95.1 1.2 %last_grads.1 = (bf16[512,256]{1,0:T(8,128)(2,1)}, bf16[512,256]{1,0:T(8,128)(2,1)}) custom-call(f32[520,128]{1,0:T(8,128)S(1)} %get-tuple-element.24.start_ref, bf16[512,256]{1,0:T(8,128)(2,1)S(1)} %copy-done.1, bf16[512,256]{1,0:T(8,128)(2,1)S(1)} %copy-done.2, f32[512,256]{1,0:T(8,128)S(1)} %get-tuple-element.37.kg_in_ref, ...), custom_call_target="tpu_custom_call" | custom-call | flops 268435456 | bytes 2625536 | tf_op jit(solution)/shard_map/last_grads/pallas_call | solution.py:318
  (2 shorter events, 0.0 us)
Async XLA Ops:
  0.6 28.9 %copy-start.4 = (s32[64]{0:T(128)S(1)}, s32[64]{0:T(128)}, u32[]{:S(2)}) copy-start(s32[64]{0:T(128)} %param.11) | copy-start | bytes 772
  0.6 34.2 %copy-start.1 = (bf16[512,256]{1,0:T(8,128)(2,1)S(1)}, bf16[512,256]{1,0:T(8,128)(2,1)}, u32[]{:S(2)}) copy-start(bf16[512,256]{1,0:T(8,128)(2,1)} %k_ref.5) | copy-start | bytes 786436
  0.7 34.2 %copy-start.2 = (bf16[512,256]{1,0:T(8,128)(2,1)S(1)}, bf16[512,256]{1,0:T(8,128)(2,1)}, u32[]{:S(2)}) copy-start(bf16[512,256]{1,0:T(8,128)(2,1)} %v_ref.5) | copy-start | bytes 786436
  0.7 34.2 %copy-start.3 = (bf16[512,256]{1,0:T(8,128)(2,1)S(1)}, bf16[512,256]{1,0:T(8,128)(2,1)}, u32[]{:S(2)}) copy-start(bf16[512,256]{1,0:T(8,128)(2,1)} %og_ref.1) | copy-start | bytes 786436
  2.8 32.0 %copy-start = (bf16[512,256]{1,0:T(8,128)(2,1)S(1)}, bf16[512,256]{1,0:T(8,128)(2,1)}, u32[]{:S(2)}) copy-start(bf16[512,256]{1,0:T(8,128)(2,1)} %q_ref.7) | copy-start | bytes 786436
  29.8 5.1 %copy-start.5 = (f32[256]{0:T(256)S(1)}, f32[256]{0:T(256)}, u32[]{:S(2)}) copy-start(f32[256]{0:T(256)} %param.10) | copy-start | bytes 3076
  29.8 6.4 %collective-permute-start = (f32[16,128]{1,0:T(8,128)S(1)}, f32[16,128]{1,0:T(8,128)S(1)}, u32[]{:S(2)}, u32[]{:S(2)}) collective-permute-start(f32[16,128]{1,0:T(8,128)S(1)} %total.2), channel_id=1, source_target_pairs={{0,256},{16,272},{32,288},{48,304},{64,320},{80,336},{96,352},{112... | collective-permute-start | bytes 24584 | tf_op jit(solution)/shard_map/ppermute | solution.py:348
  75.2 7.9 %collective-permute-start.1 = (f32[16,128]{1,0:T(8,128)S(1)}, f32[16,128]{1,0:T(8,128)S(1)}, u32[]{:S(2)}, u32[]{:S(2)}) collective-permute-start(f32[16,128]{1,0:T(8,128)S(1)} %total.3), channel_id=1, source_target_pairs={{256,0},{272,16},{288,32},{304,48},{320,64},{336,80},{352,96},{368... | collective-permute-start | bytes 24584 | tf_op jit(solution)/shard_map/ppermute | solution.py:348

commit v3 on v2

--- a/solution.py
+++ b/solution.py
@@ -23,12 +23,6 @@
     return lax.dot_general(a, b, (((ca,), (cb,)), ((), ())), preferred_element_type=F32)
 
 
-def dot_state(a, s, cs):
-    high = s.astype(BF16)
-    low = (s - high.astype(F32)).astype(BF16)
-    return dot(a, high, 1, cs) + dot(a, low, 1, cs)
-
-
 def iota(shape, dim):
     return lax.broadcasted_iota(jnp.int32, shape, dim).astype(F32)
 
@@ -57,32 +51,35 @@
     return slice(h * DH, (h + 1) * DH)
 
 
-def summary_kernel(lengths_hbm, k_hbm, v_hbm, out_ref, lengths, k_in, v_in, sems):
+def diagonal(total):
+    return [total[head(h), head(h)].reshape(8, 16, DH) for h in range(2)]
+
+
+def summary_kernel(lengths_hbm, k_hbm, v_hbm, lengths_ref, k_ref, v_ref, out_ref, sems):
     parts = range(0, TOK, CHUNK)
-    first = pltpu.make_async_copy(lengths_hbm, lengths, sems.at[0])
+    first = pltpu.make_async_copy(lengths_hbm, lengths_ref, sems.at[0])
     first.start()
     copies = []
     for n, at in enumerate(parts):
         rows = slice(at, at + CHUNK)
-        for m, (hbm, ref) in enumerate(((k_hbm, k_in), (v_hbm, v_in))):
+        for m, (hbm, ref) in enumerate(((k_hbm, k_ref), (v_hbm, v_ref))):
             copy = pltpu.make_async_copy(hbm.at[rows], ref.at[rows], sems.at[1 + 2 * n + m])
             copy.start()
             copies.append(copy)
     first.wait()
-    starts = doc_starts(lengths)
+    starts = doc_starts(lengths_ref)
     last = jnp.broadcast_to(first_token() + (TOK - 1), (8, starts.shape[1]))
     start = start_of(starts, last)[:1] - first_token()
-    totals = [0.0, 0.0]
+    total = 0.0
     for n, at in enumerate(parts):
         copies[2 * n].wait()
         copies[2 * n + 1].wait()
         rows = slice(at, at + CHUNK)
-        open_end = (iota((CHUNK, DH), 0) + at >= start).astype(F32)
-        for h in range(2):
-            k = k_in[rows, head(h)].astype(F32)
-            totals[h] = totals[h] + dot((k * open_end).astype(BF16), v_in[rows, head(h)], 0, 0)
-    for h in range(2):
-        out_ref[h * 8 : (h + 1) * 8] = totals[h].reshape(8, 16, DH)
+        open_end = (iota((CHUNK, WIDE), 0) + at >= start).astype(F32)
+        k = (k_ref[rows].astype(F32) * open_end).astype(BF16)
+        total = total + dot(k, v_ref[rows], 0, 0)
+    for h, piece in enumerate(diagonal(total)):
+        out_ref[h * 8 : (h + 1) * 8] = piece
 
 
 def keeps(starts, reverse):
@@ -165,12 +162,33 @@
             scaled_ref[where] = og_ref[where].astype(F32) * gain_ref[:, head(h)]
 
 
-def entering(start_ref, state_ref, part_ref, b, h):
-    state = state_ref[head(h), :]
-    if b == 0:
-        return state
-    keep = (start_ref[BLK - 1 : BLK, :] < first_token()).astype(F32)
-    return keep * state + part_ref[head(h), :]
+def both_heads(state):
+    zero = jnp.zeros((DH, DH), F32)
+    whole = jnp.concatenate(
+        [
+            jnp.concatenate([state[head(0)], zero], axis=1),
+            jnp.concatenate([zero, state[head(1)]], axis=1),
+        ],
+        axis=0,
+    )
+    high = whole.astype(BF16)
+    return high, (whole - high.astype(F32)).astype(BF16)
+
+
+def dot_state(a, state, cs):
+    return dot(a, state[0], 1, cs) + dot(a, state[1], 1, cs)
+
+
+def entering(start_ref, state_ref, part_ref, b):
+    state = state_ref[...]
+    if b == 1:
+        keep = (start_ref[BLK - 1 : BLK, :] < first_token()).astype(F32)
+        state = keep * state + part_ref[...]
+    return both_heads(state)
+
+
+def twice(x):
+    return jnp.concatenate([x, x], axis=1)
 
 
 def applies_fwd(start_ref, b):
@@ -182,17 +200,12 @@
 ):
     rows = []
     for b in range(2):
-        apply = applies_fwd(start_ref, b)
-        square, inner = 0.0, 0.0
-        for h in range(2):
-            where = (span(b), head(h))
-            state = entering(start_ref, state_ref, part_ref, b, h)
-            att = within_ref[where] + dot_state(q_ref[where], state, 0) * apply
-            att_ref[where] = att
-            scaled = scaled_ref[where]
-            square = square + att * att
-            inner = inner + scaled * att
-        rows.append((square, inner))
+        state = entering(start_ref, state_ref, part_ref, b)
+        across = dot_state(q_ref[span(b)], state, 0)
+        att = within_ref[span(b)] + across * twice(applies_fwd(start_ref, b))
+        att_ref[span(b)] = att
+        square, inner = att * att, scaled_ref[span(b)] * att
+        rows.append((square[:, :DH] + square[:, DH:], inner[:, :DH] + inner[:, DH:]))
     lines = []
     for which in range(2):
         for b in range(2):
@@ -213,16 +226,14 @@
 def delta_kernel(start_ref, q_ref, scaled_ref, att_ref, sums_ref, delta_ref, out_ref):
     sums = jnp.sum(sums_ref[...], axis=0)
     radius = jnp.sqrt(sums[:4] / FEAT + EPSILON)
-    inverse = tall(1.0 / radius)
-    factor = tall(sums[4:] / (FEAT * radius * radius * radius))
-    open_start = (start_ref[:TOK, :] <= first_token()).astype(F32)
-    for h in range(2):
-        delta = scaled_ref[:, head(h)] * inverse - att_ref[:, head(h)] * factor
-        delta = delta.astype(BF16)
-        delta_ref[:, head(h)] = delta
-        q = q_ref[:, head(h)].astype(F32)
-        total = dot((q * open_start).astype(BF16), delta, 0, 0)
-        out_ref[h * 8 : (h + 1) * 8] = total.reshape(8, 16, DH)
+    inverse = twice(tall(1.0 / radius))
+    factor = twice(tall(sums[4:] / (FEAT * radius * radius * radius)))
+    open_start = twice((start_ref[:TOK, :] <= first_token()).astype(F32))
+    delta = (scaled_ref[...] * inverse - att_ref[...] * factor).astype(BF16)
+    delta_ref[...] = delta
+    q = (q_ref[...].astype(F32) * open_start).astype(BF16)
+    for h, piece in enumerate(diagonal(dot(q, delta, 0, 0))):
+        out_ref[h * 8 : (h + 1) * 8] = piece
 
 
 def local_grads_kernel(
@@ -256,7 +267,9 @@
         back_ref[head(h), :] = dot((q * open_mid).astype(BF16), delta_ref[BLK:, head(h)], 0, 0)
     for b in range(2):
         mask = allowed(start_ref, b)
-        apply = applies_fwd(start_ref, b)
+        apply = twice(applies_fwd(start_ref, b))
+        state = entering(start_ref, state_ref, part_ref, b)
+        across = dot_state(delta_ref[span(b)], state, 1) * apply
         for h in range(2):
             where = (span(b), head(h))
             normed_ref[where] = (att_ref[where] * inverse[span(b)] * gain_ref[:, head(h)]).astype(
@@ -264,10 +277,7 @@
             )
             delta = delta_ref[where]
             dprobs = jnp.where(mask, dot(delta, v_ref[where], 1, 1), 0.0).astype(BF16)
-            state = entering(start_ref, state_ref, part_ref, b, h)
-            qg_ref[where] = (
-                dot(dprobs, k_ref[where], 1, 0) + dot_state(delta, state, 1) * apply
-            ).astype(BF16)
+            qg_ref[where] = (dot(dprobs, k_ref[where], 1, 0) + across[:, head(h)]).astype(BF16)
             kg_ref[where] = dot(dprobs, q_ref[where], 0, 0)
             vg_ref[where] = dot(probs_ref[2 * b + h], delta, 0, 0)
 
@@ -292,16 +302,15 @@
     for b in range(2):
         edge = (b + 1) * BLK
         at = base + b * BLK + iota((BLK, DH), 0)
-        apply = (at >= start_ref[edge : edge + 1, :]).astype(F32)
-        for h in range(2):
-            where = (span(b), head(h))
-            state = state_ref[head(h), :]
-            if b == 0:
-                state = keep * state + part_ref[head(h), :]
-            kg = kg_in_ref[where] + dot_state(v_ref[where], state, 1) * apply
-            vg = vg_in_ref[where] + dot_state(k_ref[where], state, 0) * apply
-            kg_ref[where] = kg.astype(BF16)
-            vg_ref[where] = vg.astype(BF16)
+        apply = twice((at >= start_ref[edge : edge + 1, :]).astype(F32))
+        state = state_ref[...]
+        if b == 0:
+            state = keep * state + part_ref[...]
+        state = both_heads(state)
+        kg = kg_in_ref[span(b)] + dot_state(v_ref[span(b)], state, 1) * apply
+        kg_ref[span(b)] = kg.astype(BF16)
+        vg = vg_in_ref[span(b)] + dot_state(k_ref[span(b)], state, 0) * apply
+        vg_ref[span(b)] = vg.astype(BF16)
         for i, (ref, hbm) in enumerate(((kg_ref, kg_hbm), (vg_ref, vg_hbm))):
             copy = pltpu.make_async_copy(ref.at[span(b)], hbm.at[span(b)], sems.at[b, i])
             copy.start()
@@ -357,23 +366,16 @@
     lengths = lengths.reshape(1, -1)
     gain = gain.reshape(1, -1)
     docs = lengths.shape
-    (summary,) = call(
+    lengths, k, v, summary = call(
         summary_kernel,
-        [(PIECES, F32)],
-        lengths,
-        k,
-        v,
+        [(docs, jnp.int32), (TOKENS, BF16), (TOKENS, BF16), (PIECES, F32)],
+        *(pltpu.with_memory_space_constraint(a, pltpu.HBM) for a in (lengths, k, v)),
         flops=1 << 26,
         name="summary",
-        grant=60,
         in_specs=[HBM] * 3,
-        scratch_shapes=[
-            pltpu.VMEM(docs, jnp.int32),
-            pltpu.VMEM(TOKENS, BF16),
-            pltpu.VMEM(TOKENS, BF16),
-            pltpu.SemaphoreType.DMA((1 + 2 * (TOK // CHUNK),)),
-        ],
-    )
+        scratch_shapes=[pltpu.SemaphoreType.DMA((1 + 2 * (TOK // CHUNK),))],
+    )
+    q, og, summary = lax.optimization_barrier((q, og, summary))
     x = swap(summary)
     before = total_before(lengths, x, False)
     prefix, still, start, probs, within, scaled, part = call(

time: 96.7 us -> 95.8 us (level)
  transfers between devices with their start and end apart: 2 -> 2, of which waited for: 2 -> 1; matrix products, arithmetic and copies ran while one was open for 0% -> 0% of each run, Pallas kernels for 3% -> 3%
where the time goes in v3:
time: 95.8 us; the launch traced here: 95.4 us
  blocking collectives  76.3 us (80%)
  Pallas kernels  7.11 us (7%)
  starting transfers between devices  6.95 us (7%)
  waiting for transfers between devices  3.65 us (4%)
    all_to_all x4, blocking collectives, swap(): return lax.all_to_all(x, 'ctx', 0, 0, axis_index_groups=groups)  61.8 us
    all_to_all x1, blocking collectives, body(): sums = lax.all_to_all(sums, 'head', 0, 0)  14.5 us
    pallas_call x10, Pallas kernels, call(): pl.pallas_call(kernel, out_shape=shapes, compiler_params=pltpu.CompilerPa...  7.11 us
    ppermute x2, starting transfers between devices, total_before(): return lax.ppermute(total, 'ctx', pairs)  6.95 us
    ppermute x2, waiting for transfers between devices, total_before(): return lax.ppermute(total, 'ctx', pairs)  3.65 us
  transfers between devices with their start and end apart: 2, of which 1 were waited for; matrix products, arithmetic and copies ran while one was open for 0% of the time, Pallas kernels for 3%

profile of v3, /device:TPU:32, one launch (start us, length us, event | category | flops | bytes accessed | tf_op | source)
XLA Modules:
  0.0 95.4 jit_solution(1994667341726645498)
XLA Ops:
  0.6 0.0 copy-start.1
  0.6 1.5 %summary.1 = (s32[1,64]{1,0:T(1,128)S(1)}, bf16[512,256]{1,0:T(8,128)(2,1)S(1)}, bf16[512,256]{1,0:T(8,128)(2,1)S(1)}, f32[16,16,128]{2,1,0:T(8,128)S(1)}) custom-call(s32[1,64]{1,0:T(1,128)} %bitcast.9, bf16[512,256]{1,0:T(8,128)(2,1)} %k_hbm.1, bf16[512,256]{1,0:T(8,128)(2,1)} %v_hbm.1), custom_call_target="tpu_custom_call" | custom-call | flops 67108864 | bytes 1180160 | tf_op jit(solution)/shard_map/summary/pallas_call | solution.py:327
  2.1 0.0 copy-start
  2.1 26.5 %all_to_all.25.x_ref = f32[16,16,128]{2,1,0:T(8,128)S(1)} all-to-all(f32[16,16,128]{2,1,0:T(8,128)S(1)} %get-tuple-element.33), channel_id=1, replica_groups={{0,16,32,48,64,80,96,112,128,144,160,176,192,208,224,240},{256,272,288,..., dimensions={0} | all-to-all | bytes 262144 | tf_op jit(solution)/shard_map/all_to_all | solution.py:348
  28.6 0.2 total.2
  28.8 5.0 %collective-permute-start = (f32[16,128]{1,0:T(8,128)S(1)}, f32[16,128]{1,0:T(8,128)S(1)}, u32[]{:S(2)}, u32[]{:S(2)}) collective-permute-start(f32[16,128]{1,0:T(8,128)S(1)} %total.2), channel_id=1, source_target_pairs={{0,256},{16,272},{32,288},{48,304},{64,320},{80,336},{96,352},{112... | collective-permute-start | bytes 24584 | tf_op jit(solution)/shard_map/ppermute | solution.py:357
  33.9 0.0 copy-start.2
  33.9 0.0 copy-done.1
  33.9 0.0 copy-done
  33.9 0.7 copy-done.2
  34.6 0.8 within.1
  35.4 0.0 collective-permute-done.before_ref
  35.4 11.5 %all_to_all.26 = f32[16,16,128]{2,1,0:T(8,128)S(1)} all-to-all(f32[16,16,128]{2,1,0:T(8,128)S(1)} %join.2), channel_id=1, replica_groups={{0,16,32,48,64,80,96,112,128,144,160,176,192,208,224,240},{256,272,288,..., dimensions={0} | all-to-all | bytes 262144 | tf_op jit(solution)/shard_map/all_to_all | solution.py:348
  46.9 0.5 attend.1
  47.4 14.5 %all_to_all.27.sums_ref = f32[16,8,128]{2,1,0:T(8,128)S(1)} all-to-all(f32[16,8,128]{2,1,0:T(8,128)S(1)} %get-tuple-element.45), channel_id=1, replica_groups=mesh['ctx'=64,'head'=16] {'head'}, dimensions={0} | all-to-all | bytes 131072 | tf_op jit(solution)/shard_map/all_to_all | solution.py:415
  62.0 0.5 delta.1
  62.5 11.7 %all_to_all.28.x_ref = f32[16,16,128]{2,1,0:T(8,128)S(1)} all-to-all(f32[16,16,128]{2,1,0:T(8,128)S(1)} %get-tuple-element.46), channel_id=1, replica_groups={{0,16,32,48,64,80,96,112,128,144,160,176,192,208,224,240},{256,272,288,..., dimensions={0} | all-to-all | bytes 262144 | tf_op jit(solution)/shard_map/all_to_all | solution.py:348
  74.2 0.2 total.3
  74.4 1.9 %collective-permute-start.1 = (f32[16,128]{1,0:T(8,128)S(1)}, f32[16,128]{1,0:T(8,128)S(1)}, u32[]{:S(2)}, u32[]{:S(2)}) collective-permute-start(f32[16,128]{1,0:T(8,128)S(1)} %total.3), channel_id=1, source_target_pairs={{256,0},{272,16},{288,32},{304,48},{320,64},{336,80},{352,96},{368... | collective-permute-start | bytes 24584 | tf_op jit(solution)/shard_map/ppermute | solution.py:357
  76.3 2.2 %local_grads.1 = (f32[16,16,128]{2,1,0:T(8,128)S(1)}, f32[16,128]{1,0:T(8,128)S(1)}, bf16[512,256]{1,0:T(8,128)(2,1)}, bf16[512,256]{1,0:T(8,128)(2,1)}, f32[512...) custom-call(s32[1,64]{1,0:T(1,128)S(1)} %get-tuple-element.31.lengths_ref, ...), custom_call_target="tpu_custom_call" | custom-call | flops 536870912 | bytes 4666624 | tf_op jit(solution)/shard_map/local_grads/pallas_call | solution.py:327
  78.5 3.7 %collective-permute-done.1.before_ref = f32[16,128]{1,0:T(8,128)S(1)} collective-permute-done((f32[16,128]{1,0:T(8,128)S(1)}, f32[16,128]{1,0:T(8,128)S(1)}, u32[]{:S(2)}, u32[]{:S(2)}) %collective-permute-start.1) | collective-permute-done | bytes 8224 | tf_op jit(solution)/shard_map/ppermute | solution.py:357
  82.2 12.1 %all_to_all.29 = f32[16,16,128]{2,1,0:T(8,128)S(1)} all-to-all(f32[16,16,128]{2,1,0:T(8,128)S(1)} %join.3), channel_id=1, replica_groups={{0,16,32,48,64,80,96,112,128,144,160,176,192,208,224,240},{256,272,288,..., dimensions={0} | all-to-all | bytes 262144 | tf_op jit(solution)/shard_map/all_to_all | solution.py:348
  94.2 1.2 %last_grads.1 = (bf16[512,256]{1,0:T(8,128)(2,1)}, bf16[512,256]{1,0:T(8,128)(2,1)}) custom-call(f32[520,128]{1,0:T(8,128)S(1)} %get-tuple-element.38.start_ref, bf16[512,256]{1,0:T(8,128)(2,1)S(1)} %get-tuple-element.35.k_ref, bf16[512,256]{1,0:T(8,128)(2,1)S(1)} %get-tuple-element.36.v_ref, f32[512,256]{1,0:T(8,128)S(1)} %get-tuple-element.51.kg_in_ref, ...), custom_call_target="tpu_custom_call" | custom-call | flops 268435456 | bytes 2625536 | tf_op jit(solution)/shard_map/last_grads/pallas_call | solution.py:327
  (2 shorter events, 0.0 us)
Async XLA Ops:
  0.6 33.3 %copy-start.1 = (bf16[512,256]{1,0:T(8,128)(2,1)S(1)}, bf16[512,256]{1,0:T(8,128)(2,1)}, u32[]{:S(2)}) copy-start(bf16[512,256]{1,0:T(8,128)(2,1)} %og_ref) | copy-start | bytes 786436
  2.1 31.8 %copy-start = (bf16[512,256]{1,0:T(8,128)(2,1)S(1)}, bf16[512,256]{1,0:T(8,128)(2,1)}, u32[]{:S(2)}) copy-start(bf16[512,256]{1,0:T(8,128)(2,1)} %q_ref.3) | copy-start | bytes 786436
  28.8 6.5 %collective-permute-start = (f32[16,128]{1,0:T(8,128)S(1)}, f32[16,128]{1,0:T(8,128)S(1)}, u32[]{:S(2)}, u32[]{:S(2)}) collective-permute-start(f32[16,128]{1,0:T(8,128)S(1)} %total.2), channel_id=1, source_target_pairs={{0,256},{16,272},{32,288},{48,304},{64,320},{80,336},{96,352},{112... | collective-permute-start | bytes 24584 | tf_op jit(solution)/shard_map/ppermute | solution.py:357
  33.9 0.7 copy-start.2
  74.4 7.8 %collective-permute-start.1 = (f32[16,128]{1,0:T(8,128)S(1)}, f32[16,128]{1,0:T(8,128)S(1)}, u32[]{:S(2)}, u32[]{:S(2)}) collective-permute-start(f32[16,128]{1,0:T(8,128)S(1)} %total.3), channel_id=1, source_target_pairs={{256,0},{272,16},{288,32},{304,48},{320,64},{336,80},{352,96},{368... | collective-permute-start | bytes 24584 | tf_op jit(solution)/shard_map/ppermute | solution.py:357

commit v4 on v3

--- a/solution.py
+++ b/solution.py
@@ -13,7 +13,7 @@
 EPSILON = 1e-06
 TOK = 512
 WIDE = 256
-CHUNK = 256
+CHUNK = 512
 GROUP = 16
 F32 = jnp.float32
 BF16 = jnp.bfloat16
@@ -298,23 +298,23 @@
 ):
     base = first_token()
     keep = (start_ref[TOK : TOK + 1, :] <= base + BLK).astype(F32)
-    copies = []
+    state = state_ref[...]
+    states = [both_heads(keep * state + part_ref[...]), both_heads(state)]
+    applies = []
     for b in range(2):
         edge = (b + 1) * BLK
         at = base + b * BLK + iota((BLK, DH), 0)
-        apply = twice((at >= start_ref[edge : edge + 1, :]).astype(F32))
-        state = state_ref[...]
-        if b == 0:
-            state = keep * state + part_ref[...]
-        state = both_heads(state)
-        kg = kg_in_ref[span(b)] + dot_state(v_ref[span(b)], state, 1) * apply
-        kg_ref[span(b)] = kg.astype(BF16)
-        vg = vg_in_ref[span(b)] + dot_state(k_ref[span(b)], state, 0) * apply
-        vg_ref[span(b)] = vg.astype(BF16)
-        for i, (ref, hbm) in enumerate(((kg_ref, kg_hbm), (vg_ref, vg_hbm))):
-            copy = pltpu.make_async_copy(ref.at[span(b)], hbm.at[span(b)], sems.at[b, i])
-            copy.start()
-            copies.append(copy)
+        applies.append(twice((at >= start_ref[edge : edge + 1, :]).astype(F32)))
+    copies = []
+    for i, (local, x, side, ref, hbm) in enumerate(
+        ((kg_in_ref, v_ref, 1, kg_ref, kg_hbm), (vg_in_ref, k_ref, 0, vg_ref, vg_hbm))
+    ):
+        for b in range(2):
+            across = dot_state(x[span(b)], states[b], side) * applies[b]
+            ref[span(b)] = (local[span(b)] + across).astype(BF16)
+        copy = pltpu.make_async_copy(ref, hbm, sems.at[i])
+        copy.start()
+        copies.append(copy)
     for copy in copies:
         copy.wait()
 
@@ -471,7 +471,7 @@
         scratch_shapes=[
             pltpu.VMEM(TOKENS, BF16),
             pltpu.VMEM(TOKENS, BF16),
-            pltpu.SemaphoreType.DMA((2, 2)),
+            pltpu.SemaphoreType.DMA((2,)),
         ],
     )
     return normed, qg, kg, vg

time: 95.8 us -> 95.8 us (level)
  no operation moved by 1% of the time
where the time goes in v4:
time: 95.8 us; the launch traced here: 95.4 us
  blocking collectives  76.3 us (80%)
  Pallas kernels  7.05 us (7%)
  starting transfers between devices  6.95 us (7%)
  waiting for transfers between devices  3.65 us (4%)
    all_to_all x4, blocking collectives, swap(): return lax.all_to_all(x, 'ctx', 0, 0, axis_index_groups=groups)  61.8 us
    all_to_all x1, blocking collectives, body(): sums = lax.all_to_all(sums, 'head', 0, 0)  14.5 us
    pallas_call x10, Pallas kernels, call(): pl.pallas_call(kernel, out_shape=shapes, compiler_params=pltpu.CompilerPa...  7.05 us
    ppermute x2, starting transfers between devices, total_before(): return lax.ppermute(total, 'ctx', pairs)  6.95 us
    ppermute x2, waiting for transfers between devices, total_before(): return lax.ppermute(total, 'ctx', pairs)  3.65 us
  transfers between devices with their start and end apart: 2, of which 1 were waited for; matrix products, arithmetic and copies ran while one was open for 0% of the time, Pallas kernels for 3%

profile of v4, /device:TPU:32, one launch (start us, length us, event | category | flops | bytes accessed | tf_op | source)
XLA Modules:
  0.0 95.4 jit_solution(7274560436882214545)
XLA Ops:
  0.6 0.0 copy-start.1
  0.6 1.4 %summary.1 = (s32[1,64]{1,0:T(1,128)S(1)}, bf16[512,256]{1,0:T(8,128)(2,1)S(1)}, bf16[512,256]{1,0:T(8,128)(2,1)S(1)}, f32[16,16,128]{2,1,0:T(8,128)S(1)}) custom-call(s32[1,64]{1,0:T(1,128)} %bitcast.9, bf16[512,256]{1,0:T(8,128)(2,1)} %k_hbm.1, bf16[512,256]{1,0:T(8,128)(2,1)} %v_hbm.1), custom_call_target="tpu_custom_call" | custom-call | flops 67108864 | bytes 1180160 | tf_op jit(solution)/shard_map/summary/pallas_call | solution.py:327
  2.1 0.0 copy-start
  2.1 26.5 %all_to_all.25.x_ref = f32[16,16,128]{2,1,0:T(8,128)S(1)} all-to-all(f32[16,16,128]{2,1,0:T(8,128)S(1)} %get-tuple-element.33), channel_id=1, replica_groups={{0,16,32,48,64,80,96,112,128,144,160,176,192,208,224,240},{256,272,288,..., dimensions={0} | all-to-all | bytes 262144 | tf_op jit(solution)/shard_map/all_to_all | solution.py:348
  28.6 0.2 total.2
  28.8 5.0 %collective-permute-start = (f32[16,128]{1,0:T(8,128)S(1)}, f32[16,128]{1,0:T(8,128)S(1)}, u32[]{:S(2)}, u32[]{:S(2)}) collective-permute-start(f32[16,128]{1,0:T(8,128)S(1)} %total.2), channel_id=1, source_target_pairs={{0,256},{16,272},{32,288},{48,304},{64,320},{80,336},{96,352},{112... | collective-permute-start | bytes 24584 | tf_op jit(solution)/shard_map/ppermute | solution.py:357
  33.8 0.0 copy-start.2
  33.8 0.0 copy-done.1
  33.8 0.0 copy-done
  33.9 0.7 copy-done.2
  34.5 0.8 within.1
  35.3 0.0 collective-permute-done.before_ref
  35.3 11.6 %all_to_all.26 = f32[16,16,128]{2,1,0:T(8,128)S(1)} all-to-all(f32[16,16,128]{2,1,0:T(8,128)S(1)} %join.2), channel_id=1, replica_groups={{0,16,32,48,64,80,96,112,128,144,160,176,192,208,224,240},{256,272,288,..., dimensions={0} | all-to-all | bytes 262144 | tf_op jit(solution)/shard_map/all_to_all | solution.py:348
  46.9 0.5 attend.1
  47.4 14.5 %all_to_all.27.sums_ref = f32[16,8,128]{2,1,0:T(8,128)S(1)} all-to-all(f32[16,8,128]{2,1,0:T(8,128)S(1)} %get-tuple-element.45), channel_id=1, replica_groups=mesh['ctx'=64,'head'=16] {'head'}, dimensions={0} | all-to-all | bytes 131072 | tf_op jit(solution)/shard_map/all_to_all | solution.py:415
  61.9 0.5 delta.1
  62.4 11.7 %all_to_all.28.x_ref = f32[16,16,128]{2,1,0:T(8,128)S(1)} all-to-all(f32[16,16,128]{2,1,0:T(8,128)S(1)} %get-tuple-element.46), channel_id=1, replica_groups={{0,16,32,48,64,80,96,112,128,144,160,176,192,208,224,240},{256,272,288,..., dimensions={0} | all-to-all | bytes 262144 | tf_op jit(solution)/shard_map/all_to_all | solution.py:348
  74.1 0.2 total.3
  74.3 1.9 %collective-permute-start.1 = (f32[16,128]{1,0:T(8,128)S(1)}, f32[16,128]{1,0:T(8,128)S(1)}, u32[]{:S(2)}, u32[]{:S(2)}) collective-permute-start(f32[16,128]{1,0:T(8,128)S(1)} %total.3), channel_id=1, source_target_pairs={{256,0},{272,16},{288,32},{304,48},{320,64},{336,80},{352,96},{368... | collective-permute-start | bytes 24584 | tf_op jit(solution)/shard_map/ppermute | solution.py:357
  76.2 2.2 %local_grads.1 = (f32[16,16,128]{2,1,0:T(8,128)S(1)}, f32[16,128]{1,0:T(8,128)S(1)}, bf16[512,256]{1,0:T(8,128)(2,1)}, bf16[512,256]{1,0:T(8,128)(2,1)}, f32[512...) custom-call(s32[1,64]{1,0:T(1,128)S(1)} %get-tuple-element.31.lengths_ref, ...), custom_call_target="tpu_custom_call" | custom-call | flops 536870912 | bytes 4666624 | tf_op jit(solution)/shard_map/local_grads/pallas_call | solution.py:327
  78.4 3.7 %collective-permute-done.1.before_ref = f32[16,128]{1,0:T(8,128)S(1)} collective-permute-done((f32[16,128]{1,0:T(8,128)S(1)}, f32[16,128]{1,0:T(8,128)S(1)}, u32[]{:S(2)}, u32[]{:S(2)}) %collective-permute-start.1) | collective-permute-done | bytes 8224 | tf_op jit(solution)/shard_map/ppermute | solution.py:357
  82.1 12.1 %all_to_all.29 = f32[16,16,128]{2,1,0:T(8,128)S(1)} all-to-all(f32[16,16,128]{2,1,0:T(8,128)S(1)} %join.3), channel_id=1, replica_groups={{0,16,32,48,64,80,96,112,128,144,160,176,192,208,224,240},{256,272,288,..., dimensions={0} | all-to-all | bytes 262144 | tf_op jit(solution)/shard_map/all_to_all | solution.py:348
  94.2 1.2 %last_grads.1 = (bf16[512,256]{1,0:T(8,128)(2,1)}, bf16[512,256]{1,0:T(8,128)(2,1)}) custom-call(f32[520,128]{1,0:T(8,128)S(1)} %get-tuple-element.38.start_ref, bf16[512,256]{1,0:T(8,128)(2,1)S(1)} %get-tuple-element.35.k_ref, bf16[512,256]{1,0:T(8,128)(2,1)S(1)} %get-tuple-element.36.v_ref, f32[512,256]{1,0:T(8,128)S(1)} %get-tuple-element.51.kg_in_ref, ...), custom_call_target="tpu_custom_call" | custom-call | flops 268435456 | bytes 2625536 | tf_op jit(solution)/shard_map/last_grads/pallas_call | solution.py:327
  (2 shorter events, 0.0 us)
Async XLA Ops:
  0.6 33.2 %copy-start.1 = (bf16[512,256]{1,0:T(8,128)(2,1)S(1)}, bf16[512,256]{1,0:T(8,128)(2,1)}, u32[]{:S(2)}) copy-start(bf16[512,256]{1,0:T(8,128)(2,1)} %og_ref) | copy-start | bytes 786436
  2.1 31.8 %copy-start = (bf16[512,256]{1,0:T(8,128)(2,1)S(1)}, bf16[512,256]{1,0:T(8,128)(2,1)}, u32[]{:S(2)}) copy-start(bf16[512,256]{1,0:T(8,128)(2,1)} %q_ref.3) | copy-start | bytes 786436
  28.8 6.5 %collective-permute-start = (f32[16,128]{1,0:T(8,128)S(1)}, f32[16,128]{1,0:T(8,128)S(1)}, u32[]{:S(2)}, u32[]{:S(2)}) collective-permute-start(f32[16,128]{1,0:T(8,128)S(1)} %total.2), channel_id=1, source_target_pairs={{0,256},{16,272},{32,288},{48,304},{64,320},{80,336},{96,352},{112... | collective-permute-start | bytes 24584 | tf_op jit(solution)/shard_map/ppermute | solution.py:357
  33.8 0.7 copy-start.2
  74.3 7.8 %collective-permute-start.1 = (f32[16,128]{1,0:T(8,128)S(1)}, f32[16,128]{1,0:T(8,128)S(1)}, u32[]{:S(2)}, u32[]{:S(2)}) collective-permute-start(f32[16,128]{1,0:T(8,128)S(1)} %total.3), channel_id=1, source_target_pairs={{256,0},{272,16},{288,32},{304,48},{320,64},{336,80},{352,96},{368... | collective-permute-start | bytes 24584 | tf_op jit(solution)/shard_map/ppermute | solution.py:357

commit v5 on v4

--- a/solution.py
+++ b/solution.py
@@ -132,8 +132,8 @@
     q_ref,
     k_ref,
     v_ref,
-    og_ref,
-    gain_ref,
+    og_hbm,
+    gain_hbm,
     prefix_ref,
     open_ref,
     start_ref,
@@ -141,7 +141,16 @@
     within_ref,
     scaled_ref,
     part_ref,
+    og_ref,
+    gain_ref,
+    sems,
 ):
+    copies = [
+        pltpu.make_async_copy(og_hbm, og_ref, sems.at[0]),
+        pltpu.make_async_copy(gain_hbm, gain_ref, sems.at[1]),
+    ]
+    for copy in copies:
+        copy.start()
     starts = doc_starts(lengths_ref)
     group_prefix(False, starts, x_ref, prefix_ref, open_ref)
     positions = first_token() + iota((TOK + 8, starts.shape[1]), 0)
@@ -159,7 +168,9 @@
             probs = jnp.where(mask, scores, 0.0).astype(BF16)
             probs_ref[2 * b + h] = probs
             within_ref[where] = dot(probs, v_ref[where], 1, 0)
-            scaled_ref[where] = og_ref[where].astype(F32) * gain_ref[:, head(h)]
+    for copy in copies:
+        copy.wait()
+    scaled_ref[...] = og_ref[...].astype(F32) * gain_ref[...]
 
 
 def both_heads(state):
@@ -394,10 +405,15 @@
         q,
         k,
         v,
-        og,
-        gain,
+        *(pltpu.with_memory_space_constraint(a, pltpu.HBM) for a in (og, gain)),
         flops=1 << 28,
         name="within",
+        in_specs=[VMEM] * 5 + [HBM] * 2,
+        scratch_shapes=[
+            pltpu.VMEM(TOKENS, BF16),
+            pltpu.VMEM((1, WIDE), F32),
+            pltpu.SemaphoreType.DMA((2,)),
+        ],
     )
     state = joined(prefix, still, before)
     att, sums = call(

time: 95.8 us -> 95.7 us (level)
  transfers between devices with their start and end apart: 2 -> 2, of which waited for: 1 -> 2; matrix products, arithmetic and copies ran while one was open for 0% -> 0% of each run, Pallas kernels for 3% -> 4%
where the time goes in v5:
time: 95.7 us; the launch traced here: 95.3 us
  blocking collectives  76.3 us (80%)
  Pallas kernels  7.52 us (8%)
  starting transfers between devices  6.95 us (7%)
  waiting for transfers between devices  3.14 us (3%)
    all_to_all x4, blocking collectives, swap(): return lax.all_to_all(x, 'ctx', 0, 0, axis_index_groups=groups)  61.8 us
    all_to_all x1, blocking collectives, body(): sums = lax.all_to_all(sums, 'head', 0, 0)  14.5 us
    pallas_call x10, Pallas kernels, call(): pl.pallas_call(kernel, out_shape=shapes, compiler_params=pltpu.CompilerPa...  7.52 us
    ppermute x2, starting transfers between devices, total_before(): return lax.ppermute(total, 'ctx', pairs)  6.95 us
    ppermute x2, waiting for transfers between devices, total_before(): return lax.ppermute(total, 'ctx', pairs)  3.14 us
  transfers between devices with their start and end apart: 2, of which 2 were waited for; matrix products, arithmetic and copies ran while one was open for 0% of the time, Pallas kernels for 4%

profile of v5, /device:TPU:32, one launch (start us, length us, event | category | flops | bytes accessed | tf_op | source)
XLA Modules:
  0.0 95.3 jit_solution(9433425860937530657)
XLA Ops:
  0.6 1.4 %summary.1 = (s32[1,64]{1,0:T(1,128)S(1)}, bf16[512,256]{1,0:T(8,128)(2,1)S(1)}, bf16[512,256]{1,0:T(8,128)(2,1)S(1)}, f32[16,16,128]{2,1,0:T(8,128)S(1)}) custom-call(s32[1,64]{1,0:T(1,128)} %bitcast.9, bf16[512,256]{1,0:T(8,128)(2,1)} %k_hbm.1, bf16[512,256]{1,0:T(8,128)(2,1)} %v_hbm.1), custom_call_target="tpu_custom_call" | custom-call | flops 67108864 | bytes 1180160 | tf_op jit(solution)/shard_map/summary/pallas_call | solution.py:338
  2.0 0.0 copy-start
  2.0 26.5 %all_to_all.25.x_ref = f32[16,16,128]{2,1,0:T(8,128)S(1)} all-to-all(f32[16,16,128]{2,1,0:T(8,128)S(1)} %get-tuple-element.33), channel_id=1, replica_groups={{0,16,32,48,64,80,96,112,128,144,160,176,192,208,224,240},{256,272,288,..., dimensions={0} | all-to-all | bytes 262144 | tf_op jit(solution)/shard_map/all_to_all | solution.py:359
  28.5 0.2 total.2
  28.7 5.0 %collective-permute-start = (f32[16,128]{1,0:T(8,128)S(1)}, f32[16,128]{1,0:T(8,128)S(1)}, u32[]{:S(2)}, u32[]{:S(2)}) collective-permute-start(f32[16,128]{1,0:T(8,128)S(1)} %total.2), channel_id=1, source_target_pairs={{0,256},{16,272},{32,288},{48,304},{64,320},{80,336},{96,352},{112... | collective-permute-start | bytes 24584 | tf_op jit(solution)/shard_map/ppermute | solution.py:368
  33.8 0.0 copy-done
  33.8 1.3 %within.1 = (f32[16,16,128]{2,1,0:T(8,128)S(1)}, f32[16,128]{1,0:T(8,128)S(1)}, f32[520,128]{1,0:T(8,128)S(1)}, bf16[4,256,256]{2,1,0:T(8,128)(2,1)S(1)}, f32[51...) custom-call(s32[1,64]{1,0:T(1,128)S(1)} %get-tuple-element.31.lengths_ref, ...), custom_call_target="tpu_custom_call" | custom-call | flops 268435456 | bytes 3290368 | tf_op jit(solution)/shard_map/within/pallas_call | solution.py:338
  35.1 0.1 collective-permute-done.before_ref
  35.2 11.5 %all_to_all.26 = f32[16,16,128]{2,1,0:T(8,128)S(1)} all-to-all(f32[16,16,128]{2,1,0:T(8,128)S(1)} %join.2), channel_id=1, replica_groups={{0,16,32,48,64,80,96,112,128,144,160,176,192,208,224,240},{256,272,288,..., dimensions={0} | all-to-all | bytes 262144 | tf_op jit(solution)/shard_map/all_to_all | solution.py:359
  46.7 0.5 attend.1
  47.2 14.5 %all_to_all.27.sums_ref = f32[16,8,128]{2,1,0:T(8,128)S(1)} all-to-all(f32[16,8,128]{2,1,0:T(8,128)S(1)} %get-tuple-element.45), channel_id=1, replica_groups=mesh['ctx'=64,'head'=16] {'head'}, dimensions={0} | all-to-all | bytes 131072 | tf_op jit(solution)/shard_map/all_to_all | solution.py:431
  61.8 0.5 delta.1
  62.3 11.7 %all_to_all.28.x_ref = f32[16,16,128]{2,1,0:T(8,128)S(1)} all-to-all(f32[16,16,128]{2,1,0:T(8,128)S(1)} %get-tuple-element.46), channel_id=1, replica_groups={{0,16,32,48,64,80,96,112,128,144,160,176,192,208,224,240},{256,272,288,..., dimensions={0} | all-to-all | bytes 262144 | tf_op jit(solution)/shard_map/all_to_all | solution.py:359
  74.0 0.2 total.3
  74.2 1.9 %collective-permute-start.1 = (f32[16,128]{1,0:T(8,128)S(1)}, f32[16,128]{1,0:T(8,128)S(1)}, u32[]{:S(2)}, u32[]{:S(2)}) collective-permute-start(f32[16,128]{1,0:T(8,128)S(1)} %total.3), channel_id=1, source_target_pairs={{256,0},{272,16},{288,32},{304,48},{320,64},{336,80},{352,96},{368... | collective-permute-start | bytes 24584 | tf_op jit(solution)/shard_map/ppermute | solution.py:368
  76.1 0.0 copy-start.1
  76.1 0.7 copy-done.1
  76.8 2.2 %local_grads.1 = (f32[16,16,128]{2,1,0:T(8,128)S(1)}, f32[16,128]{1,0:T(8,128)S(1)}, bf16[512,256]{1,0:T(8,128)(2,1)}, bf16[512,256]{1,0:T(8,128)(2,1)}, f32[512...) custom-call(s32[1,64]{1,0:T(1,128)S(1)} %get-tuple-element.31.lengths_ref, ...), custom_call_target="tpu_custom_call" | custom-call | flops 536870912 | bytes 4666624 | tf_op jit(solution)/shard_map/local_grads/pallas_call | solution.py:338
  79.0 3.1 %collective-permute-done.1.before_ref = f32[16,128]{1,0:T(8,128)S(1)} collective-permute-done((f32[16,128]{1,0:T(8,128)S(1)}, f32[16,128]{1,0:T(8,128)S(1)}, u32[]{:S(2)}, u32[]{:S(2)}) %collective-permute-start.1) | collective-permute-done | bytes 8224 | tf_op jit(solution)/shard_map/ppermute | solution.py:368
  82.1 12.1 %all_to_all.29 = f32[16,16,128]{2,1,0:T(8,128)S(1)} all-to-all(f32[16,16,128]{2,1,0:T(8,128)S(1)} %join.3), channel_id=1, replica_groups={{0,16,32,48,64,80,96,112,128,144,160,176,192,208,224,240},{256,272,288,..., dimensions={0} | all-to-all | bytes 262144 | tf_op jit(solution)/shard_map/all_to_all | solution.py:359
  94.1 1.2 %last_grads.1 = (bf16[512,256]{1,0:T(8,128)(2,1)}, bf16[512,256]{1,0:T(8,128)(2,1)}) custom-call(f32[520,128]{1,0:T(8,128)S(1)} %get-tuple-element.38.start_ref, bf16[512,256]{1,0:T(8,128)(2,1)S(1)} %get-tuple-element.35.k_ref, bf16[512,256]{1,0:T(8,128)(2,1)S(1)} %get-tuple-element.36.v_ref, f32[512,256]{1,0:T(8,128)S(1)} %get-tuple-element.51.kg_in_ref, ...), custom_call_target="tpu_custom_call" | custom-call | flops 268435456 | bytes 2625536 | tf_op jit(solution)/shard_map/last_grads/pallas_call | solution.py:338
  (2 shorter events, 0.0 us)
Async XLA Ops:
  2.0 31.8 %copy-start = (bf16[512,256]{1,0:T(8,128)(2,1)S(1)}, bf16[512,256]{1,0:T(8,128)(2,1)}, u32[]{:S(2)}) copy-start(bf16[512,256]{1,0:T(8,128)(2,1)} %q_ref.3) | copy-start | bytes 786436
  28.7 6.4 %collective-permute-start = (f32[16,128]{1,0:T(8,128)S(1)}, f32[16,128]{1,0:T(8,128)S(1)}, u32[]{:S(2)}, u32[]{:S(2)}) collective-permute-start(f32[16,128]{1,0:T(8,128)S(1)} %total.2), channel_id=1, source_target_pairs={{0,256},{16,272},{32,288},{48,304},{64,320},{80,336},{96,352},{112... | collective-permute-start | bytes 24584 | tf_op jit(solution)/shard_map/ppermute | solution.py:368
  74.2 7.9 %collective-permute-start.1 = (f32[16,128]{1,0:T(8,128)S(1)}, f32[16,128]{1,0:T(8,128)S(1)}, u32[]{:S(2)}, u32[]{:S(2)}) collective-permute-start(f32[16,128]{1,0:T(8,128)S(1)} %total.3), channel_id=1, source_target_pairs={{256,0},{272,16},{288,32},{304,48},{320,64},{336,80},{352,96},{368... | collective-permute-start | bytes 24584 | tf_op jit(solution)/shard_map/ppermute | solution.py:368
  76.1 0.7 copy-start.1
